TPU v7x, 32 devices: a whole 2x2x4 slice. The times are simulated.
32 devices in a mesh: dp: 8 (over z, y), aa: 2 (over x), ba: 2 (over core).
Axes of the slice: x: 2, y: 2, z: 4, core: 2. Of those that a mesh axis runs over, the one named last changes fastest.
Arguments:
- images: bfloat16 [192, 196, 768], P(('dp', 'ba'), None, 'aa'), may hold values from -6 to 6
- counts: int32 [16], P(('dp', 'ba')), may hold values from 6 to 12, as said below
- ln1_gain: float32 [768], P('aa'), may hold values from 0.5 to 1.5
- ln1_bias: float32 [768], P('aa'), may hold values from -1.75 to 1.75
- tok_w1: bfloat16 [196, 384], replicated, may hold values from -0.4375 to 0.4375
- tok_b1: float32 [384], replicated, may hold values from -1.75 to 1.75
- tok_w2: bfloat16 [384, 196], replicated, may hold values from -0.3125 to 0.3125
- tok_b2: float32 [196], replicated, may hold values from -1.75 to 1.75
- ln2_gain: float32 [768], P('aa'), may hold values from 0.5 to 1.5
- ln2_bias: float32 [768], P('aa'), may hold values from -1.75 to 1.75
- ch_w1: bfloat16 [768, 3072], P(None, 'ba'), may hold values from -0.21875 to 0.21875
- ch_b1: float32 [3072], P('ba'), may hold values from -1.75 to 1.75
- ch_w2: bfloat16 [3072, 768], P('ba'), may hold values from -0.109375 to 0.109375
- ch_b2: float32 [768], P('aa'), may hold values from -1.75 to 1.75
- cotangent: bfloat16 [192, 196, 768], P(('dp', 'ba'), None, 'aa'), may hold values from -6 to 6
Outputs:
- output: bfloat16 [192, 196, 768], P(('dp', 'ba'), None, 'aa')
- grad_images: float32 [192, 196, 768], P(('dp', 'ba'), None, 'aa')
- grad_ln1_gain: float32 [768], P('aa')
- grad_ln1_bias: float32 [768], P('aa')
- grad_tok_w1: float32 [196, 384], replicated
- grad_tok_b1: float32 [384], replicated
- grad_tok_w2: float32 [384, 196], replicated
- grad_tok_b2: float32 [196], replicated
- grad_ln2_gain: float32 [768], P('aa')
- grad_ln2_bias: float32 [768], P('aa')
- grad_ch_w1: float32 [768, 3072], P(None, 'ba')
- grad_ch_b1: float32 [3072], P('ba')
- grad_ch_w2: float32 [3072, 768], P('ba')
- grad_ch_b2: float32 [768], P('aa')
Inputs may be any that keep to these rules, and one draw needn't show every extreme that they name: Group g of 12 slots holds counts[g] real images in its first slots; at least one group is full in every draw.
All inputs are finite; a program needn't handle non-finite values.
Results may differ from a plain program's by a relative error of at most 0.007.
Values may be sent and summed in bfloat16 or wider, within the bound.
A program may use at most 192 MiB of HBM per device.

v0:
```python
import jax
import jax.numpy as jnp
from jax import lax
from jax.sharding import PartitionSpec as P

D = 768


epsilon = 1e-06


def norm_forward(values, gain_vec, bias_vec):
    row_sums = lax.psum(jnp.sum(values, -1), "aa")
    centered = values - (row_sums / D)[..., None]
    spread = lax.psum(jnp.sum(centered * centered, -1), "aa") / D
    inv_std = lax.rsqrt(spread + epsilon)[..., None]
    normed = centered * inv_std
    return (normed * gain_vec + bias_vec, normed, inv_std)


def norm_backward(upstream, normed, inv_std, gain_vec):
    scaled = upstream * gain_vec
    mean_grad, proj_grad = lax.psum((jnp.sum(scaled, -1), jnp.sum(scaled * normed, -1)), "aa")
    return inv_std * (scaled - (mean_grad / D)[..., None] - normed * (proj_grad / D)[..., None])


def return_rows(partial_value):
    halves = lax.psum_scatter(partial_value, "ba", scatter_dimension=0, tiled=True)
    back_rows = lax.psum_scatter(halves, "aa", scatter_dimension=1, tiled=True)
    return back_rows


def contract_rows(left, right):
    return lax.dot_general(
        left, right, (((0,), (0,)), ((), ())), preferred_element_type=jnp.float32
    )


def contract_last(left, right):
    return lax.dot_general(
        left, right, (((1,), (1,)), ((), ())), preferred_element_type=jnp.float32
    )


def local(
    images,
    counts,
    ln1_gain,
    ln1_bias,
    tok_w1,
    tok_b1,
    tok_w2,
    tok_b2,
    ln2_gain,
    ln2_bias,
    ch_w1,
    ch_b1,
    ch_w2,
    ch_b2,
    cotangent,
):
    num_img, patches, channels = images.shape
    row_count = num_img * patches
    slot_ids = lax.broadcasted_iota(jnp.int32, (num_img, 1, 1), 0)
    valid = (slot_ids < counts[0]).astype(jnp.float32)
    source = images.astype(jnp.float32)
    y1_full, normed_one, inv_one = norm_forward(source, ln1_gain, ln1_bias)
    y1_low = y1_full.astype(jnp.bfloat16)
    pre_tok = (
        jnp.einsum("sk,isc->ikc", tok_w1, y1_low, preferred_element_type=jnp.float32)
        + tok_b1[None, :, None]
    )
    act_tok, back_tok = jax.vjp(jax.nn.gelu, pre_tok)
    act_tok_low = act_tok.astype(jnp.bfloat16)
    token_out = (
        jnp.einsum("ks,ikc->isc", tok_w2, act_tok_low, preferred_element_type=jnp.float32)
        + tok_b2[None, :, None]
    )
    residual = source + token_out
    y2_full, normed_two, inv_two = norm_forward(residual, ln2_gain, ln2_bias)
    y2_rows = y2_full.astype(jnp.bfloat16).reshape(row_count, channels)
    grad_out = (valid * cotangent.astype(jnp.float32)).astype(jnp.bfloat16)
    grad_rows = grad_out.reshape(row_count, channels)
    hidden_w = ch_w1.shape[1]
    arrived = (
        lax.all_gather(y2_rows, "aa", axis=1, tiled=True),
        lax.all_gather(grad_rows, "aa", axis=1, tiled=True),
    )
    cols_dev = hidden_w // lax.axis_size("aa")
    col_start = lax.axis_index("aa") * cols_dev
    paired_in, paired_grad = (
        lax.all_gather(arrived[0], "ba", axis=0, tiled=True),
        lax.all_gather(arrived[1], "ba", axis=0, tiled=True),
    )
    w_in = lax.dynamic_slice_in_dim(ch_w1, col_start, cols_dev, 1)
    b_in = lax.dynamic_slice_in_dim(ch_b1, col_start, cols_dev, 0)
    w_out = lax.dynamic_slice_in_dim(ch_w2, col_start, cols_dev, 0)
    pre_chan = jnp.dot(paired_in, w_in, preferred_element_type=jnp.float32) + b_in
    act_chan, back_chan = jax.vjp(jax.nn.gelu, pre_chan)
    act_chan_low = act_chan.astype(jnp.bfloat16)
    chan_out = return_rows(jnp.dot(act_chan_low, w_out, preferred_element_type=jnp.float32))
    chan_out = chan_out.reshape(num_img, patches, channels)
    output = (valid * (residual + chan_out + ch_b2)).astype(jnp.bfloat16)
    grad_act_chan = contract_last(paired_grad, w_out)
    grad_pre_chan = back_chan(grad_act_chan)[0].astype(jnp.bfloat16)
    part_w_out = contract_rows(act_chan_low, paired_grad)
    part_w_in = contract_rows(paired_in, grad_pre_chan)
    part_b_in = jnp.sum(grad_pre_chan.astype(jnp.float32), 0)
    grad_y2 = return_rows(contract_last(grad_pre_chan, w_in)).reshape(num_img, patches, channels)
    grad_out_full = grad_out.astype(jnp.float32)
    grad_bias_chan = jnp.sum(grad_out_full, (0, 1))
    grad_gain_two = jnp.sum(grad_y2 * normed_two, (0, 1))
    grad_bias_two = jnp.sum(grad_y2, (0, 1))
    grad_residual = grad_out_full + norm_backward(grad_y2, normed_two, inv_two, ln2_gain)
    grad_tok = grad_residual.astype(jnp.bfloat16)
    grad_tok_w2 = jnp.einsum(
        "ikc,isc->ks", act_tok_low, grad_tok, preferred_element_type=jnp.float32
    )
    grad_tok_b2 = jnp.sum(grad_tok.astype(jnp.float32), (0, 2))
    grad_act_tok = jnp.einsum("ks,isc->ikc", tok_w2, grad_tok, preferred_element_type=jnp.float32)
    grad_pre_tok = back_tok(grad_act_tok)[0].astype(jnp.bfloat16)
    grad_tok_w1 = jnp.einsum(
        "isc,ikc->sk", y1_low, grad_pre_tok, preferred_element_type=jnp.float32
    )
    grad_tok_b1 = jnp.sum(grad_pre_tok.astype(jnp.float32), (0, 2))
    grad_y1 = jnp.einsum("sk,ikc->isc", tok_w1, grad_pre_tok, preferred_element_type=jnp.float32)
    grad_gain_one = jnp.sum(grad_y1 * normed_one, (0, 1))
    grad_bias_one = jnp.sum(grad_y1, (0, 1))
    grad_images = grad_residual + norm_backward(grad_y1, normed_one, inv_one, ln1_gain)
    sum_tw1, sum_tb1, sum_tw2, sum_tb2 = lax.psum(
        (grad_tok_w1, grad_tok_b1, grad_tok_w2, grad_tok_b2), ("dp", "aa", "ba")
    )
    sum_g1, sum_b1, sum_g2, sum_b2, sum_cb2 = lax.psum(
        (grad_gain_one, grad_bias_one, grad_gain_two, grad_bias_two, grad_bias_chan), ("dp", "ba")
    )
    local_w1, local_b1, local_w2 = lax.psum((part_w_in, part_b_in, part_w_out), "dp")
    sum_cw1, sum_cb1, sum_cw2 = (
        lax.all_gather(local_w1, "aa", axis=1, tiled=True),
        lax.all_gather(local_b1, "aa", axis=0, tiled=True),
        lax.all_gather(local_w2, "aa", axis=0, tiled=True),
    )
    return (
        output,
        grad_images,
        sum_g1,
        sum_b1,
        sum_tw1,
        sum_tb1,
        sum_tw2,
        sum_tb2,
        sum_g2,
        sum_b2,
        sum_cw1,
        sum_cb1,
        sum_cw2,
        sum_cb2,
    )


def solution(mesh):
    placed = (
        P(("dp", "ba"), None, "aa"),
        P(("dp", "ba")),
        P("aa"),
        P("aa"),
        P(),
        P(),
        P(),
        P(),
        P("aa"),
        P("aa"),
        P(None, "ba"),
        P("ba"),
        P("ba", None),
        P("aa"),
        P(("dp", "ba"), None, "aa"),
    )
    return jax.shard_map(
        local,
        mesh=mesh,
        in_specs=placed,
        out_specs=(
            P(("dp", "ba"), None, "aa"),
            P(("dp", "ba"), None, "aa"),
            P("aa"),
            P("aa"),
            P(),
            P(),
            P(),
            P(),
            P("aa"),
            P("aa"),
            P(None, "ba"),
            P("ba"),
            P("ba", None),
            P("aa"),
        ),
        check_vma=False,
    )
```

profile of v0, /device:TPU:0, one launch (start us, length us, event | category | flops | bytes accessed | tf_op | source)
XLA Modules:
  0.0 1016.0 jit_solution(5389693442290880054)
XLA Ops:
  9.4 9.7 psum.140
  37.9 8.8 psum.142
  71.3 44.1 %all-gather.8.cloned.1.call-done = bf16[2352,768]{1,0:T(8,128)(2,1)} async-done(((bf16[2352,384]{1,0:T(8,128)(2,1)}), bf16[2352,768]{1,0:T(8,128)(2,1)}) %all-gather.8.cloned.1.call-update) | async-done | bytes 3612688 | tf_op jit(solution)/shard_map/all_gather | solution.py:86
  115.5 52.3 %all-gather.12.cloned.1.call-done = bf16[2352,768]{1,0:T(8,128)(2,1)} async-done(((bf16[2352,384]{1,0:T(8,128)(2,1)}), bf16[2352,768]{1,0:T(8,128)(2,1)}) %all-gather.12.cloned.1.call-update) | async-done | bytes 3612688 | tf_op jit(solution)/shard_map/all_gather | solution.py:87
  168.1 19.4 %all-gather.10.cloned.1.call-done = bf16[4704,768]{1,0:T(8,128)(2,1)} async-done(((bf16[2352,768]{1,0:T(8,128)(2,1)}), bf16[4704,768]{1,0:T(8,128)(2,1)}) %all-gather.10.cloned.1.call-update) | async-done | bytes 7225360 | tf_op jit(solution)/shard_map/all_gather | solution.py:92
  187.5 15.3 %multiply_convert_fusion = (bf16[4704,768]{1,0:T(8,128)(2,1)}, f32[4704,768]{1,0:T(8,128)}) fusion(f32[768]{0:T(1024)S(1)} %dynamic_slice.10, bf16[4704,768]{1,0:T(8,128)(2,1)} %all-gather.10.cloned.1.call-done, bf16[768,1536]{1,0:T(8,128)(2,1)S(1)} %copy-done, s32[]{:T(128)S(6)} %select_n.2), kind=kOutput, calls=%fused_computation.10 | convolution fusion | flops 5585190912 | bytes 30085124 | tf_op jit(solution)/shard_map/dot_general | solution.py:98
  208.2 11.5 %fusion.62 = f32[768,768]{1,0:T(8,128)} fusion(bf16[4704,768]{1,0:T(8,128)(2,1)} %get-tuple-element.43, bf16[4704,768]{1,0:T(8,128)(2,1)} %all-gather.14.cloned.1.call-done), kind=kOutput, calls=%fused_computation.92 | convolution fusion | flops 5549064192 | bytes 16809984 | tf_op jit(solution)/shard_map/dot_general | solution.py:34
  219.7 20.4 %convert_reduce_fusion = (f32[768]{0:T(1024)S(1)}, bf16[4704,768]{1,0:T(8,128)(2,1)}) fusion(f32[4704,768]{1,0:T(8,128)} %get-tuple-element.44, f32[768]{0:T(1024)S(1)} %dynamic_slice.10, bf16[4704,768]{1,0:T(8,128)(2,1)} %all-gather.14.cloned.1.call-done, bf16[1536,768]{1,0:T(8,128)(2,1)S(1)} %copy-done.21, s32[]{:T(128)S(6)} %select_n.2), kind=kOutput, calls=%fused_computation.9 | convolution fusion | flops 5632154624 | bytes 30088196 | tf_op jit(solution)/shard_map/dot_general | solution.py:40
  240.1 10.6 %fusion.61 = f32[768,768]{1,0:T(8,128)} fusion(bf16[4704,768]{1,0:T(8,128)(2,1)S(1)} %bitcast.76, bf16[4704,768]{1,0:T(8,128)(2,1)} %get-tuple-element.49), kind=kOutput, calls=%fused_computation.91 | convolution fusion | flops 5549064192 | bytes 16809984 | tf_op jit(solution)/shard_map/dot_general | solution.py:34
  250.8 12.2 %fusion.39 = f32[4704,768]{1,0:T(8,128)} fusion(bf16[4704,768]{1,0:T(8,128)(2,1)} %get-tuple-element.49, bf16[768,1536]{1,0:T(8,128)(2,1)S(1)} %copy-done, s32[]{:T(128)S(6)} %select_n.2), kind=kOutput, calls=%fused_computation.64 | convolution fusion | flops 5549064192 | bytes 22855684 | tf_op jit(solution)/shard_map/dot_general | solution.py:40
  264.7 11.8 %fusion.35 = f32[4704,768]{1,0:T(8,128)} fusion(bf16[4704,768]{1,0:T(8,128)(2,1)} %get-tuple-element.43, bf16[1536,768]{1,0:T(8,128)(2,1)S(1)} %copy-done.22, s32[]{:T(128)S(6)} %select_n.2), kind=kOutput, calls=%fused_computation.62 | convolution fusion | flops 5549064192 | bytes 22855684 | tf_op jit(solution)/shard_map/dot_general | solution.py:101
  276.6 145.5 %all-reduce.11.cloned.1.call-done = (f32[768,768]{1,0:T(8,128)}, f32[768,768]{1,0:T(8,128)}) async-done(((f32[768,768]{1,0:T(8,128)}, f32[768,768]{1,0:T(8,128)}), (f32[768,768]{1,0:T(8,128)}, f32[768,768]{1,0:T(8,128)})) %all-reduce.11.cloned.1.call-update) | async-done | bytes 4718608 | tf_op jit(solution)/shard_map/psum | solution.py:136
  422.9 24.0 %reduce-scatter.9.cloned.1.call-done = f32[2352,768]{1,0:T(8,128)} async-done(((f32[4704,768]{1,0:T(8,128)}), f32[2352,768]{1,0:T(8,128)}) %reduce-scatter.9.cloned.1.call-update) | async-done | bytes 7225360 | tf_op jit(solution)/shard_map/reduce_scatter | solution.py:28
  447.0 27.3 %reduce-scatter.5.cloned.1.call-done = f32[2352,768]{1,0:T(8,128)} async-done(((f32[4704,768]{1,0:T(8,128)}), f32[2352,768]{1,0:T(8,128)}) %reduce-scatter.5.cloned.1.call-update) | async-done | bytes 7225360 | tf_op jit(solution)/shard_map/reduce_scatter | solution.py:28
  474.3 21.7 %psum.157 = f32[768]{0:T(1024)S(1)} all-reduce(f32[768]{0:T(1024)S(1)} %get-tuple-element.48), channel_id=1, replica_groups=mesh['dp'=8,'aa'=2,'ba'=2] {'dp'}, use_global_device_ids=true, to_apply=%region_36.0 | all-reduce | flops 768 | bytes 6144 | tf_op jit(solution)/shard_map/psum | solution.py:136
  501.1 38.7 %all-gather.16.cloned.1.call-done = f32[768,1536]{1,0:T(8,128)} async-done(((f32[768,768]{1,0:T(8,128)}), f32[768,1536]{1,0:T(8,128)}) %all-gather.16.cloned.1.call-update) | async-done | bytes 4718608 | tf_op jit(solution)/shard_map/all_gather | solution.py:138
  539.8 64.2 %all-gather.18.cloned.1.call-done = f32[1536,768]{1,0:T(8,128)} async-done(((f32[768,768]{1,0:T(8,128)}), f32[1536,768]{1,0:T(8,128)}) %all-gather.18.cloned.1.call-update) | async-done | bytes 4718608 | tf_op jit(solution)/shard_map/all_gather | solution.py:140
  604.1 89.4 %reduce-scatter.11.cloned.1.call-done = f32[2352,384]{1,0:T(8,128)} async-done(((f32[2352,768]{1,0:T(8,128)}), f32[2352,384]{1,0:T(8,128)}) %reduce-scatter.11.cloned.1.call-update) | async-done | bytes 3612688 | tf_op jit(solution)/shard_map/reduce_scatter | solution.py:29
  705.8 7.8 all-reduce.5
  713.7 70.0 %reduce-scatter.7.cloned.1.call-done = f32[2352,384]{1,0:T(8,128)} async-done(((f32[2352,768]{1,0:T(8,128)}), f32[2352,384]{1,0:T(8,128)}) %reduce-scatter.7.cloned.1.call-update) | async-done | bytes 3612688 | tf_op jit(solution)/shard_map/reduce_scatter | solution.py:29
  795.7 8.0 convolution_bitcast_fusion
  826.8 40.5 %all-reduce = (f32[384]{0:T(512)}, f32[196]{0:T(256)}) all-reduce(f32[384]{0:T(512)S(1)} %get-tuple-element.46, f32[196]{0:T(256)S(1)} %get-tuple-element.36), channel_id=1, replica_groups=mesh['dp'=8,'aa'=2,'ba'=2] {'dp','aa','ba'}, use_global_device_ids=true, to_apply=%region_26.0 | all-reduce | flops 580 | bytes 4640 | tf_op jit(solution)/shard_map/psum | solution.py:130
  869.7 59.6 %all-reduce.2 = (f32[384]{0:T(512)}, f32[384]{0:T(512)}, f32[384]{0:T(512)}, f32[384]{0:T(512)}, f32[384]{0:T(512)}) all-reduce(f32[384]{0:T(512)S(1)} %get-tuple-element.16, f32[384]{0:T(512)S(1)} %reduce_sum.156, f32[384]{0:T(512)S(1)} %get-tuple-element.14, ...), channel_id=1, replica_groups=mesh['dp'=8,'aa'=2,'ba'=2] {'dp','ba'}, use_global_device_ids=true, to_apply=%region_21.0 | all-reduce | flops 1920 | bytes 15360 | tf_op jit(solution)/shard_map/psum | solution.py:133
  935.6 59.8 %all-reduce.9.cloned.1.call-done = (f32[196,384]{1,0:T(8,128)}, f32[384,196]{0,1:T(8,128)}) async-done(((f32[196,384]{1,0:T(8,128)}, f32[384,196]{0,1:T(8,128)}), (f32[196,384]{1,0:T(8,128)}, f32[384,196]{0,1:T(8,128)})) %all-reduce.9.cloned.1.call-update) | async-done | bytes 602128 | tf_op jit(solution)/shard_map/psum | solution.py:130
  (129 shorter events, 127.7 us)
Async XLA Ops:
  7.2 180.3 %copy-start = (bf16[768,1536]{1,0:T(8,128)(2,1)S(1)}, bf16[768,1536]{1,0:T(8,128)(2,1)}, u32[]{:S(2)}) copy-start(bf16[768,1536]{1,0:T(8,128)(2,1)} %param.25) | copy-start | bytes 7077892
  7.2 21.6 %copy-start.14 = (f32[384]{0:T(512)S(1)}, f32[384]{0:T(512)}, u32[]{:S(2)}) copy-start(f32[384]{0:T(512)} %param.17) | copy-start | bytes 4612
  7.2 21.6 %copy-start.9 = (bf16[196,384]{1,0:T(8,128)(2,1)S(1)}, bf16[196,384]{1,0:T(8,128)(2,1)}, u32[]{:S(2)}) copy-start(bf16[196,384]{1,0:T(8,128)(2,1)} %param.19) | copy-start | bytes 451588
  7.2 21.6 %copy-start.17 = (f32[384]{0:T(512)S(1)}, f32[384]{0:T(512)}, u32[]{:S(2)}) copy-start(f32[384]{0:T(512)} %param.18) | copy-start | bytes 4612
  7.2 108.2 %all-gather.8.cloned.1.call-start = ((), (), s32[]{:S(2)}) async-start(), calls=%async_computation.4 | async-start | bytes 5419008 | tf_op jit(solution)/shard_map/all_gather | solution.py:86
  37.9 18.4 %copy-start.13 = (f32[384]{0:T(512)S(1)}, f32[384]{0:T(512)}, u32[]{:S(2)}) copy-start(f32[384]{0:T(512)} %param.23) | copy-start | bytes 4612
  37.9 18.4 %copy-start.16 = (f32[384]{0:T(512)S(1)}, f32[384]{0:T(512)}, u32[]{:S(2)}) copy-start(f32[384]{0:T(512)} %param.24) | copy-start | bytes 4612
  63.4 104.4 %all-gather.12.cloned.1.call-start = ((), (), s32[]{:S(2)}) async-start(), calls=%async_computation.8 | async-start | bytes 5419008 | tf_op jit(solution)/shard_map/all_gather | solution.py:87
  71.2 96.7 %copy-start.19 = (f32[1536]{0:T(1024)S(1)}, f32[1536]{0:T(1024)}, u32[]{:S(2)}) copy-start(f32[1536]{0:T(1024)} %param.26) | copy-start | bytes 18436
  71.3 116.2 %all-gather.10.cloned.1.call-start = ((), (), s32[]{:S(2)}) async-start(), calls=%async_computation.5 | async-start | bytes 10838016 | tf_op jit(solution)/shard_map/all_gather | solution.py:92
  115.4 92.8 %all-gather.14.cloned.1.call-start = ((), (), s32[]{:S(2)}) async-start(), calls=%async_computation.9 | async-start | bytes 10838016 | tf_op jit(solution)/shard_map/all_gather | solution.py:93
  167.8 254.3 %all-reduce.11.cloned.1.call-start = ((), (), s32[]{:S(2)}) async-start(), calls=%async_computation.15 | async-start | bytes 9437184 | tf_op jit(solution)/shard_map/psum | solution.py:136
  208.2 31.9 %slice-start.2 = ((s8[7225344]{0:T(1024)(128)(4,1)}), s8[4194304]{0:T(1024)(128)(4,1)S(1)}, s32[]{:S(2)}) async-start(s8[7225344]{0:T(1024)(128)(4,1)} %bitcast.75), calls=%async_computation.18 | async-start | bytes 8388608
  219.7 20.4 %slice-start.3 = ((s8[7225344]{0:T(1024)(128)(4,1)}), s8[3031040]{0:T(1024)(128)(4,1)S(1)}, s32[]{:S(2)}) async-start(s8[7225344]{0:T(1024)(128)(4,1)} %bitcast.75), calls=%async_computation.19 | async-start | bytes 6062080
  250.8 196.1 %reduce-scatter.9.cloned.1.call-start = ((), (), s32[]{:S(2)}) async-start(), calls=%async_computation.10 | async-start | bytes 21676032 | tf_op jit(solution)/shard_map/reduce_scatter | solution.py:28
  263.1 211.2 %reduce-scatter.5.cloned.1.call-start = ((), (), s32[]{:S(2)}) async-start(), calls=%async_computation.6 | async-start | bytes 21676032 | tf_op jit(solution)/shard_map/reduce_scatter | solution.py:28
  276.5 263.3 %all-gather.16.cloned.1.call-start = ((), (), s32[]{:S(2)}) async-start(), calls=%async_computation.12 | async-start | bytes 7077888 | tf_op jit(solution)/shard_map/all_gather | solution.py:138
  422.1 181.9 %all-gather.18.cloned.1.call-start = ((), (), s32[]{:S(2)}) async-start(), calls=%async_computation.13 | async-start | bytes 7077888 | tf_op jit(solution)/shard_map/all_gather | solution.py:140
  422.8 270.6 %reduce-scatter.11.cloned.1.call-start = ((), (), s32[]{:S(2)}) async-start(), calls=%async_computation.11 | async-start | bytes 10838016 | tf_op jit(solution)/shard_map/reduce_scatter | solution.py:29
  446.9 336.8 %reduce-scatter.7.cloned.1.call-start = ((), (), s32[]{:S(2)}) async-start(), calls=%async_computation.7 | async-start | bytes 10838016 | tf_op jit(solution)/shard_map/reduce_scatter | solution.py:29
  474.3 521.2 %all-reduce.9.cloned.1.call-start = ((), (), s32[]{:S(2)}) async-start(), calls=%async_computation.14 | async-start | bytes 1228800 | tf_op jit(solution)/shard_map/psum | solution.py:130
  713.7 74.8 %copy-start.4 = (bf16[12,196,384]{2,1,0:T(8,128)(2,1)S(1)}, bf16[12,196,384]{2,1,0:T(8,128)(2,1)}, u32[]{:S(2)}) copy-start(bf16[12,196,384]{2,1,0:T(8,128)(2,1)} %get-tuple-element.39) | copy-start | bytes 5419012
  713.7 74.8 %copy-start.20 = (f32[384]{0:T(512)S(1)}, f32[384]{0:T(512)}, u32[]{:S(2)}) copy-start(f32[384]{0:T(512)} %param.28) | copy-start | bytes 4612
  788.4 15.3 %slice-start = ((s8[7077888]{0:T(1024)(128)(4,1)}), s8[4194304]{0:T(1024)(128)(4,1)S(1)}, s32[]{:S(2)}) async-start(s8[7077888]{0:T(1024)(128)(4,1)} %bitcast.73), calls=%async_computation.16 | async-start | bytes 8388608
  (19 other events, 118.8 us)
Sparse Core Ops, SparseCore 0:
  63.5 51.8 all-gather.7
  117.5 50.1 all-gather.11
  169.3 18.1 all-gather.9
  188.9 19.2 all-gather.13
  250.9 171.1 all-reduce.10
  424.3 22.5 reduce-scatter.8
  449.3 24.8 reduce-scatter.4
  475.8 63.9 all-gather.15
  541.4 62.6 all-gather.17
  606.2 87.1 reduce-scatter.10
  695.8 87.8 reduce-scatter.6
  867.4 127.9 all-reduce.8
where the time goes:
time: 1020 us
  waiting for transfers between devices  641 us (63%)
  blocking collectives  173 us (17%)
  matrix products  113 us (11%)
  other arithmetic  37.9 us (4%)
  local copies, waits for them, and re-layouts  34.9 us (3%)
  between operations  15.7 us (2%)
    reduce_scatter x2, waiting for transfers between devices, return_rows(): back_rows = lax.psum_scatter(halves, 'aa', scatter_dimension=1, tiled=True)  159 us
    psum x1, waiting for transfers between devices, local(): lax.psum((part_w_in, part_b_in, part_w_out), 'dp')  146 us
    all_gather x1, waiting for transfers between devices, local(): lax.all_gather(local_w2, 'aa', axis=0, tiled=True)  64.2 us
    psum x1, waiting for transfers between devices, local(): lax.psum((grad_tok_w1, grad_tok_b1, grad_tok_w2, grad_tok_b2), ('dp', 'aa...  59.8 us
    psum x1, blocking collectives, local(): lax.psum((grad_gain_one, grad_bias_one, grad_gain_two, grad_bias_two, gra...  59.6 us
    all_gather x1, waiting for transfers between devices, local(): lax.all_gather(grad_rows, 'aa', axis=1, tiled=True)  52.3 us
    reduce_scatter x2, waiting for transfers between devices, return_rows(): lax.psum_scatter(partial_value, 'ba', scatter_dimension=0, tiled=True)  51.3 us
    all_gather x1, waiting for transfers between devices, local(): lax.all_gather(y2_rows, 'aa', axis=1, tiled=True)  44.1 us
  transfers between devices with their start and end apart: 12, of which 12 were waited for; matrix products, arithmetic and copies ran while one was open for 7% of the time, Pallas kernels for 0%

commit v1 on v0

v1 whole, which is shorter than its diff:
```python
import functools

import jax
import jax.numpy as jnp
from jax import lax
from jax.experimental import pallas as pl
from jax.experimental.pallas import tpu as pltpu
from jax.sharding import PartitionSpec as P

MESH = pl.DeviceIdType.MESH
EPS = 1e-06
C0 = 0.7978845608028654
C1 = C0 * 0.044715
RING = 8
LOOK = 2
F32 = jnp.float32
BF16 = jnp.bfloat16


def dot(left, right, left_dim, right_dim):
    return lax.dot_general(
        left, right, (((left_dim,), (right_dim,)), ((), ())), preferred_element_type=F32
    )


def gelu(v):
    return v * (0.5 * jnp.tanh(v * (C0 + C1 * (v * v))) + 0.5)


def gelu_both(v):
    v2 = v * v
    h = 0.5 * jnp.tanh(v * (C0 + C1 * v2)) + 0.5
    return v * h, h + (h - h * h) * (v * (2 * C0 + 6 * C1 * v2))


def mod(v):
    return lax.rem(v + 2 * RING, RING)


def layer_kernel(
    groups,
    valid,
    images,
    cot,
    vec_own,
    tw1,
    tb1,
    tw2,
    tb2,
    w1_own,
    w2_own,
    b1_own,
    out_o,
    gim_o,
    d2_o,
    d1_o,
    small_o,
    xb,
    cb,
    y2b,
    gb,
    res,
    acc,
    w1b,
    w2b,
    act,
    dg,
    stat,
    pb,
    bar,
    rs,
    xs,
    vecb,
    b1h,
    b1v,
    vacc,
    loc_x,
    snd_x,
    rcv_x,
    loc_c,
    snd_c,
    rcv_c,
    loc_w,
    snd_w,
    rcv_w,
    snd_b,
    rcv_b,
    snd_r,
    rcv_r,
    snd_e,
    rcv_e,
    snd_g,
    rcv_g,
    loc_g,
    loc_o,
    snd_o,
    rcv_o,
    loc_i,
    snd_i,
    rcv_i,
):
    imgs, patches, chans = xb.shape
    half = chans // 2
    pad = y2b.shape[0] // imgs
    piece = w1_own.shape[1]
    sub = piece // 2
    dp, aa, ba = lax.axis_index("dp"), lax.axis_index("aa"), lax.axis_index("ba")
    lo, hi = lax.rem(dp, RING), lax.div(dp, RING)
    fold = lax.rem(lo, 2)
    pos = jnp.where(fold == 0, lax.div(lo, 2), RING - 1 - lax.div(lo, 2))

    def at(place):
        place = mod(place)
        return hi * RING + jnp.where(
            place < RING // 2, 2 * place, 2 * (RING - 1 - place) + 1
        )

    dev_x = (dp, 1 - aa, ba)
    dev_c = (dp, aa, 1 - ba)
    dev_ring = ((at(pos + 1), aa, ba), (at(pos - 1), aa, ba))
    dev_hi = []
    step = 1
    while step < groups:
        partner = hi + step - 2 * step * lax.rem(lax.div(hi, step), 2)
        dev_hi.append((partner * RING + lo, aa, ba))
        step *= 2
    peers = [dev_x, dev_c, *dev_ring, *dev_hi]
    barrier = pltpu.get_barrier_semaphore()
    for peer in peers:
        pl.semaphore_signal(barrier, inc=1, device_id=peer, device_id_type=MESH)
    pl.semaphore_wait(barrier, len(peers))

    mine = pl.ds(pl.multiple_of(aa * half, half), half)
    other = pl.ds(pl.multiple_of((1 - aa) * half, half), half)
    rows_mine = pl.ds(pl.multiple_of(ba * piece, 64), piece)
    rows_other = pl.ds(pl.multiple_of((1 - ba) * piece, 64), piece)

    def remote(src, dst, send, recv, dev):
        return pltpu.make_async_remote_copy(
            src_ref=src,
            dst_ref=dst,
            send_sem=send,
            recv_sem=recv,
            device_id=dev,
            device_id_type=MESH,
        )

    def local_in(src, dst, sem, i):
        return pltpu.make_async_copy(src.at[aa * imgs + i], dst.at[i, :, mine], sem.at[i])

    def give(src, dst, send, recv, i):
        return remote(
            src.at[(1 - aa) * imgs + i], dst.at[i, :, mine], send.at[i], recv.at[i], dev_x
        )

    def take(src, dst, send, recv, i):
        return remote(
            src.at[(1 - aa) * imgs + i], dst.at[i, :, other], send.at[i], recv.at[i], dev_x
        )

    vec_copy = remote(vec_own, vecb.at[aa], snd_w.at[2], rcv_w.at[2], dev_x)
    vec_copy.start()
    vecb[aa] = vec_own[...]
    for i in range(imgs):
        local_in(images, xb, loc_x, i).start()
    for i in range(LOOK):
        give(images, xb, snd_x, rcv_x, i).start()
    b1_copy = remote(b1_own, b1h.at[ba], snd_w.at[3], rcv_w.at[3], dev_c)
    b1_copy.start()
    b1h[ba] = b1_own[...]
    w_local = []
    w_remote = []
    for k, (src, dst) in enumerate(((w1_own, w1b), (w2_own, w2b))):
        w_local.append(pltpu.make_async_copy(src, dst.at[:, rows_mine, :], loc_w.at[k]))
        w_remote.append(
            remote(src, dst.at[:, rows_mine, :], snd_w.at[k], rcv_w.at[k], dev_c)
        )
        w_local[-1].start()
        w_remote[-1].start()
    for i in range(imgs):
        local_in(cot, cb, loc_c, i).start()
    y2b[...] = jnp.zeros(y2b.shape, BF16)
    gb[...] = jnp.zeros(gb.shape, BF16)
    rs[0] = jnp.zeros(rs.shape[1:], BF16)
    vacc[...] = jnp.zeros(vacc.shape, F32)
    small_o[...] = jnp.zeros(small_o.shape, F32)
    remote(vec_own, vecb.at[1 - aa], snd_w.at[2], rcv_w.at[2], dev_x).wait()

    def vec(k):
        return jnp.concatenate([vecb[0, k : k + 1, :], vecb[1, k : k + 1, :]], axis=1)

    def token_forward(i, carry):
        local_in(images, xb, loc_x, i).wait()
        take(images, xb, snd_x, rcv_x, i).wait()

        @pl.when(i + LOOK < imgs)
        def _():
            give(images, xb, snd_x, rcv_x, i + LOOK).start()

        @pl.when(i + LOOK >= imgs)
        def _():
            give(cot, cb, snd_c, rcv_c, i + LOOK - imgs).start()

        x = xb[i].astype(F32)
        mean = jnp.mean(x, -1, keepdims=True)
        xc = x - mean
        rstd = lax.rsqrt(jnp.mean(xc * xc, -1, keepdims=True) + EPS)
        stat[0, i] = mean
        stat[1, i] = rstd
        y1 = (xc * rstd * vec(0) + vec(1)).astype(BF16)
        hid = gelu(dot(tw1[...], y1, 0, 0) + tb1[...]).astype(BF16)
        row = x + dot(tw2[...], hid, 0, 0) + tb2[...]
        res[i] = row
        mean = jnp.mean(row, -1, keepdims=True)
        xc = row - mean
        rstd = lax.rsqrt(jnp.mean(xc * xc, -1, keepdims=True) + EPS)
        stat[2, i] = mean
        stat[3, i] = rstd
        y2 = (xc * rstd * vec(2) + vec(3)).astype(BF16)
        y2b[pl.ds(pl.multiple_of(i * pad, 16), patches), :] = y2
        return carry

    lax.fori_loop(0, imgs, token_forward, 0)
    for i in range(LOOK, imgs):
        give(cot, cb, snd_c, rcv_c, i).start()

    remote(b1_own, b1h.at[1 - ba], snd_w.at[3], rcv_w.at[3], dev_c).wait()
    b1v[...] = jnp.concatenate([b1h[0], b1h[1]], axis=1)
    for k, (src, dst) in enumerate(((w1_own, w1b), (w2_own, w2b))):
        w_local[k].wait()
        remote(src, dst.at[:, rows_other, :], snd_w.at[k], rcv_w.at[k], dev_c).wait()

    chunks = 3
    size = y2b.shape[0] // chunks
    width = 2 * piece

    def chan_forward(k, carry):
        pair = lax.div(k, chunks)
        rows = pl.ds(pl.multiple_of(lax.rem(k, chunks) * size, 16), size)
        win = w1b[pl.ds(2 * pair, 2)].reshape(2 * width, chans)
        wout = w2b[pl.ds(2 * pair, 2)].reshape(2 * width, chans)
        bias = jnp.concatenate(
            [b1v[pl.ds(2 * pair, 1), :], b1v[pl.ds(2 * pair + 1, 1), :]], axis=1
        )
        val, der = gelu_both(dot(y2b[rows, :], win, 1, 1) + bias)
        val = val.astype(BF16)
        der = der.astype(BF16)
        act[2 * pair, rows, :] = val[:, :width]
        act[2 * pair + 1, rows, :] = val[:, width:]
        dg[2 * pair, rows, :] = der[:, :width]
        dg[2 * pair + 1, rows, :] = der[:, width:]
        new = dot(val, wout, 1, 0)
        acc[rows, :] = jnp.where(pair == 0, 0.0, acc[rows, :]) + new
        return carry

    lax.fori_loop(0, RING // 2 * chunks, chan_forward, 0)

    def out_local(i):
        return pltpu.make_async_copy(cb.at[i, :, mine], out_o.at[aa * imgs + i], loc_o.at[i])

    def out_remote(i, sender):
        return remote(
            cb.at[i, :, other], out_o.at[sender * imgs + i], snd_o.at[i], rcv_o.at[i], dev_x
        )

    def finish_out(i, carry):
        local_in(cot, cb, loc_c, i).wait()
        take(cot, cb, snd_c, rcv_c, i).wait()
        rows = pl.ds(pl.multiple_of(i * pad, 16), patches)
        scale = valid[aa * imgs + i]
        gb[rows, :] = (cb[i].astype(F32) * scale).astype(BF16)
        cb[i] = (scale * (res[i] + acc[rows, :] + vec(4))).astype(BF16)
        out_local(i).start()
        out_remote(i, aa).start()
        return carry

    lax.fori_loop(0, imgs, finish_out, 0)

    def to_core(par, a):
        return remote(
            pb.at[par, a, rows_other, :], bar.at[par, a], snd_b.at[par, a], rcv_b.at[par, a], dev_c
        )

    def to_ring(s, a, c):
        rows = pl.ds(c * sub, sub)
        return remote(
            rs.at[s, a, rows, :],
            rs.at[s + 1, a, rows, :],
            snd_r.at[s, a, c],
            rcv_r.at[s, a, c],
            dev_ring[a],
        )

    def chan_backward(s, carry):
        par = lax.rem(s, 2)

        @pl.when(s >= 2)
        def _():
            for a in range(2):
                to_core(par, a).wait_send()

        right = mod(pos - 1 - s)
        left = mod(pos + 1 + s)
        pb[par, 0] = dot(act[right], gb[...], 0, 0).astype(BF16)
        to_core(par, 0).start()
        grad = (dot(gb[...], w2b[left], 1, 1) * dg[left].astype(F32)).astype(BF16)
        small_o[pl.ds(416 + left, 1), :] = jnp.sum(grad.astype(F32), 0, keepdims=True)
        pb[par, 1] = dot(grad, y2b[...], 0, 0).astype(BF16)
        to_core(par, 1).start()
        acc[...] = jnp.where(s == 0, 0.0, acc[...]) + dot(grad, w1b[left], 1, 0)
        for a in range(2):
            to_core(par, a).wait_recv()
        for c in range(2):
            for a in range(2):

                @pl.when(s > 0)
                def _():
                    to_ring(s - 1, a, c).wait_recv()

                rows = pl.ds(c * sub, sub)
                own = pl.ds(pl.multiple_of(ba * piece + c * sub, 32), sub)
                total = (
                    pb[par, a, own, :].astype(F32)
                    + bar[par, a, rows, :].astype(F32)
                    + rs[s, a, rows, :].astype(F32)
                )
                rs[s, a, rows, :] = total.astype(BF16)

                @pl.when(s < RING - 1)
                def _():
                    to_ring(s, a, c).start()

        return carry

    lax.fori_loop(0, RING, chan_backward, 0)
    for par in range(2):
        for a in range(2):
            to_core(par, a).wait_send()

    last = RING - 1
    for k, dev in enumerate([dev_x, *dev_hi]):
        copies = [
            remote(rs.at[last, a], xs.at[k, a], snd_e.at[k, a], rcv_e.at[k, a], dev)
            for a in range(2)
        ]
        for copy in copies:
            copy.start()
        for a, copy in enumerate(copies):
            copy.wait()
            rs[last, a] = (rs[last, a].astype(F32) + xs[k, a].astype(F32)).astype(BF16)

    results = (d2_o, d1_o)

    def gather(t, a, c, src):
        q = mod(pos - t) if a == 0 else mod(pos + t)
        rows = pl.ds(c * sub, sub)
        dst = results[a].at[q, rows, :]
        return remote(
            dst if src is None else src.at[rows, :],
            dst,
            snd_g.at[t, a, c],
            rcv_g.at[t, a, c],
            dev_ring[a],
        )

    def gather_arrival(t, a, c):
        q = mod(pos - 1 - t) if a == 0 else mod(pos + 1 + t)
        dst = results[a].at[q, pl.ds(c * sub, sub), :]
        return remote(dst, dst, snd_g.at[t, a, c], rcv_g.at[t, a, c], dev_ring[a])

    keep = []
    for a in range(2):
        for c in range(2):
            gather(0, a, c, rs.at[last, a]).start()
        keep.append(
            pltpu.make_async_copy(rs.at[last, a], results[a].at[pos], loc_g.at[a])
        )
        keep[-1].start()

    def grad_local(i):
        return pltpu.make_async_copy(xb.at[i, :, mine], gim_o.at[aa * imgs + i], loc_i.at[i])

    def grad_remote(i, sender):
        return remote(
            xb.at[i, :, other], gim_o.at[sender * imgs + i], snd_i.at[i], rcv_i.at[i], dev_x
        )

    ones = jnp.ones((8, chans), BF16)

    def token_backward(i, carry):
        rows = pl.ds(pl.multiple_of(i * pad, 16), patches)
        up = acc[rows, :]
        grad_out = gb[rows, :].astype(F32)
        rstd = stat[3, i]
        normed = (res[i] - stat[2, i]) * rstd
        vacc[2:3, :] += jnp.sum(up * normed, 0, keepdims=True)
        vacc[3:4, :] += jnp.sum(up, 0, keepdims=True)
        vacc[4:5, :] += jnp.sum(grad_out, 0, keepdims=True)
        q = up * vec(2)
        mean = jnp.mean(q, -1, keepdims=True)
        proj = jnp.mean(q * normed, -1, keepdims=True)
        grad_res = grad_out + rstd * (q - mean - normed * proj)
        grad_tok = grad_res.astype(BF16)
        rstd = stat[1, i]
        normed = (xb[i].astype(F32) - stat[0, i]) * rstd
        y1 = (normed * vec(0) + vec(1)).astype(BF16)
        val, der = gelu_both(dot(tw1[...], y1, 0, 0) + tb1[...])
        small_o[200 : 200 + patches, :] += dot(grad_tok, val.astype(BF16), 1, 1)
        small_o[408:416, 0:patches] += dot(ones, grad_tok, 1, 1)
        grad_pre = (dot(tw2[...], grad_tok, 1, 0) * der).astype(BF16)
        small_o[0:patches, :] += dot(y1, grad_pre, 1, 1)
        small_o[400:408, :] += dot(ones, grad_pre, 1, 1)
        up = dot(tw1[...], grad_pre, 1, 0)
        vacc[0:1, :] += jnp.sum(up * normed, 0, keepdims=True)
        vacc[1:2, :] += jnp.sum(up, 0, keepdims=True)
        q = up * vec(0)
        mean = jnp.mean(q, -1, keepdims=True)
        proj = jnp.mean(q * normed, -1, keepdims=True)
        xb[i] = (grad_res + rstd * (q - mean - normed * proj)).astype(BF16)
        grad_local(i).start()
        grad_remote(i, aa).start()
        return carry

    def gather_step(t, carry):
        @pl.when(t < imgs)
        def _():
            token_backward(t, 0)

        for c in range(2):
            for a in range(2):
                gather_arrival(t, a, c).wait_recv()

                @pl.when(t + 1 < RING - 1)
                def _():
                    gather(t + 1, a, c, None).start()

        return carry

    lax.fori_loop(0, RING - 1, gather_step, 0)
    small_o[424:432, :] = vacc[:, :half]
    small_o[432:440, :] = vacc[:, half:]

    for copy in keep:
        copy.wait()

    def drain_images(i, carry):
        out_local(i).wait()
        out_remote(i, 1 - aa).wait()
        grad_local(i).wait()
        grad_remote(i, 1 - aa).wait()
        return carry

    lax.fori_loop(0, imgs, drain_images, 0)

    def drain_ring(t, carry):
        for a in range(2):
            for c in range(2):
                to_ring(t, a, c).wait_send()
                gather_arrival(t, a, c).wait_send()
        return carry

    lax.fori_loop(0, RING - 1, drain_ring, 0)


def local(groups, images, counts, ln1_gain, ln1_bias, tok_w1, tok_b1, tok_w2, tok_b2,
          ln2_gain, ln2_bias, ch_w1, ch_b1, ch_w2, ch_b2, cotangent):
    slots, patches, half = images.shape
    chans = 2 * half
    imgs = slots // 2
    pad = -(-patches // 16) * 16
    hidden = ch_w1.shape[1]
    piece = hidden // RING
    hid_tok = tok_w1.shape[1]
    valid = (jnp.arange(slots) < counts[0]).astype(F32)
    zero = jnp.zeros_like(ln1_gain)
    vec = jnp.stack([ln1_gain, ln1_bias, ln2_gain, ln2_bias, ch_b2, zero, zero, zero])
    w1 = ch_w1.T.reshape(RING, piece, chans)
    w2 = ch_w2.reshape(RING, piece, chans)
    b1 = ch_b1.reshape(RING, piece)
    steps = 1
    while 2**(steps - 1) < groups:
        steps += 1
    vmem = pl.BlockSpec(memory_space=pltpu.VMEM)
    hbm = pl.BlockSpec(memory_space=pl.ANY)
    dma = pltpu.SemaphoreType.DMA
    per_image = [dma((imgs,))] * 3
    out, gim, d2, d1, small = pl.pallas_call(
        functools.partial(layer_kernel, groups),
        out_shape=[
            jax.ShapeDtypeStruct((slots, patches, half), BF16),
            jax.ShapeDtypeStruct((slots, patches, half), BF16),
            jax.ShapeDtypeStruct((RING, piece, chans), BF16),
            jax.ShapeDtypeStruct((RING, piece, chans), BF16),
            jax.ShapeDtypeStruct((512, hid_tok), F32),
        ],
        in_specs=[pl.BlockSpec(memory_space=pltpu.SMEM), hbm, hbm]
        + [vmem] * 5
        + [hbm] * 2
        + [vmem],
        out_specs=[hbm] * 4 + [vmem],
        scratch_shapes=[
            pltpu.VMEM((imgs, patches, chans), BF16),
            pltpu.VMEM((imgs, patches, chans), BF16),
            pltpu.VMEM((imgs * pad, chans), BF16),
            pltpu.VMEM((imgs * pad, chans), BF16),
            pltpu.VMEM((imgs, patches, chans), F32),
            pltpu.VMEM((imgs * pad, chans), F32),
            pltpu.VMEM((RING, 2 * piece, chans), BF16),
            pltpu.VMEM((RING, 2 * piece, chans), BF16),
            pltpu.VMEM((RING, imgs * pad, 2 * piece), BF16),
            pltpu.VMEM((RING, imgs * pad, 2 * piece), BF16),
            pltpu.VMEM((4, imgs, patches, 1), F32),
            pltpu.VMEM((2, 2, 2 * piece, chans), BF16),
            pltpu.VMEM((2, 2, piece, chans), BF16),
            pltpu.VMEM((RING, 2, piece, chans), BF16),
            pltpu.VMEM((steps, 2, piece, chans), BF16),
            pltpu.VMEM((2, 8, half), F32),
            pltpu.VMEM((2, RING, piece), F32),
            pltpu.VMEM((RING, 2 * piece), F32),
            pltpu.VMEM((8, chans), F32),
            *per_image,
            *per_image,
            dma((2,)),
            dma((4,)),
            dma((4,)),
            dma((2, 2)),
            dma((2, 2)),
            dma((RING, 2, 2)),
            dma((RING, 2, 2)),
            dma((steps, 2)),
            dma((steps, 2)),
            dma((RING, 2, 2)),
            dma((RING, 2, 2)),
            dma((2,)),
            *per_image,
            *per_image,
        ],
        compiler_params=pltpu.CompilerParams(
            collective_id=0, has_side_effects=True, vmem_limit_bytes=63 * 2**20
        ),
    )(
        valid,
        images,
        cotangent,
        vec,
        tok_w1,
        tok_b1[:, None],
        tok_w2,
        tok_b2[:, None],
        w1,
        w2,
        b1,
    )
    small = lax.psum(small, ("dp", "aa", "ba"))
    aa, ba = lax.axis_index("aa"), lax.axis_index("ba")
    rows = lax.dynamic_slice_in_dim(small, 424 + 8 * aa, 8, 0)
    grad_b1 = lax.dynamic_slice_in_dim(small[416:424], ba * piece, piece, 1).reshape(hidden)
    return (
        out,
        gim.astype(F32),
        rows[0],
        rows[1],
        small[0:patches],
        small[400],
        small[200 : 200 + patches].T,
        small[408, :patches],
        rows[2],
        rows[3],
        d1.reshape(hidden, chans).T.astype(F32),
        grad_b1,
        d2.reshape(hidden, chans).astype(F32),
        rows[4],
    )


def solution(mesh):
    rows = P(("dp", "ba"), None, "aa")
    chan = P("aa")
    placed = (rows, P(("dp", "ba")), chan, chan, P(), P(), P(), P(), chan, chan,
              P(None, "ba"), P("ba"), P("ba", None), chan, rows)
    given = (rows, rows, chan, chan, P(), P(), P(), P(), chan, chan,
             P(None, "ba"), P("ba"), P("ba", None), chan)
    return jax.shard_map(
        functools.partial(local, mesh.shape["dp"] // RING),
        mesh=mesh,
        in_specs=placed,
        out_specs=given,
        check_vma=False,
    )
```

time: 1020 us -> 330 us (0.32)
  waiting for transfers between devices: 641 us -> 111 us
  blocking collectives: 173 us -> 0 us
  Pallas kernels: 0 us -> 170 us
  matrix products: 113 us -> 0 us
  other arithmetic: 37.9 us -> 11 us
  local copies, waits for them, and re-layouts: 34.9 us -> 21.5 us
    all_gather x6 -> x0, waiting for transfers between devices: 224 us -> none  [the longest x1 64.2 us: local(): lax.all_gather(local_w2, 'aa', axis=0, tiled=True)]
    reduce_scatter x4 -> x0, waiting for transfers between devices: 211 us -> none  [the longest x2 159 us: return_rows(): back_rows = lax.psum_scatter(halves, 'aa', scatter_dimension=1, tiled=True)]
    pallas_call x0 -> x1, Pallas kernels: none -> 170 us  [local(): pl.pallas_call(functools.partial(layer_kernel, groups), out_shape=[jax.Sh...]
    psum x9 -> x0, blocking collectives: 169 us -> none  [the longest x1 59.6 us: local(): lax.psum((grad_gain_one, grad_bias_one, grad_gain_two, grad_bias_two, gra...]
    dot_general x12 -> x0, matrix products: 113 us -> none  [the longest x2 32.6 us: contract_last(): lax.dot_general(left, right, (((1,), (1,)), ((), ())), preferred_element_...]
    psum x2 -> x1, waiting for transfers between devices: 205 us -> 111 us  [local(): small = lax.psum(small, ('dp', 'aa', 'ba'))]
    reduce_sum x8 -> x0, other arithmetic: 28.1 us -> none  [the longest x1 7.2 us: local(): grad_tok_b2 = jnp.sum(grad_tok.astype(jnp.float32), (0, 2))]
    unnamed x68 -> x22, local copies, waits for them, and re-layouts: 18 us -> 2.1 us
  transfers between devices with their start and end apart: 12 -> 1, of which waited for: 12 -> 1; matrix products, arithmetic and copies ran while one was open for 7% -> 5% of each run, Pallas kernels for 0% -> 0%
where the time goes in v1:
time: 330 us; the launch traced here: 329 us
  Pallas kernels  170 us (52%)
  waiting for transfers between devices  111 us (34%)
  local copies, waits for them, and re-layouts  21.5 us (7%)
  between operations  14.8 us (4%)
  other arithmetic  11 us (3%)
    pallas_call x1, Pallas kernels, local(): pl.pallas_call(functools.partial(layer_kernel, groups), out_shape=[jax.Sh...  170 us
    psum x1, waiting for transfers between devices, local(): small = lax.psum(small, ('dp', 'aa', 'ba'))  111 us
    convert_element_type x1, other arithmetic, local(): d2.reshape(hidden, chans).astype(F32)  6.79 us
  transfers between devices with their start and end apart: 1, of which 1 were waited for; matrix products, arithmetic and copies ran while one was open for 5% of the time, Pallas kernels for 0%

profile of v1, /device:TPU:0, one launch (start us, length us, event | category | flops | bytes accessed | tf_op | source)
XLA Modules:
  0.0 329.3 jit_solution(12293321753703926389)
XLA Ops:
  7.2 0.0 all-reduce.2.cloned.1.call-start
  7.3 4.4 %copy.32 = bf16[1536,768]{1,0:T(8,128)(2,1)} copy(bf16[1536,768]{0,1:T(8,128)(2,1)} %bitcast.18) | data formatting | bytes 4718592 | tf_op jit(solution)/shard_map/transpose | solution.py:477
  11.7 0.0 copy-done.3
  11.7 0.8 broadcast_in_dim.8.tb1
  12.5 0.8 copy.34.tw2
  13.3 0.8 copy.35.tb2
  14.2 0.0 copy-done.2
  14.2 0.7 reshape.48.b1_own
  15.5 0.5 compare_convert_fusion.valid
  16.0 0.6 stack.27.vec_own
  16.6 170.5 %shard_map.254 = (bf16[12,196,384]{2,1,0:T(8,128)(2,1)}, bf16[12,196,384]{2,1,0:T(8,128)(2,1)}, bf16[8,192,768]{2,1,0:T(8,128)(2,1)}, bf16[8,192,768]{2,1,0:T(8,128)(2,1)}, f32[512,384]{1,0:T(8,128)}) custom-call(f32[12]{0:T(128)} %compare_convert_fusion.valid, bf16[12,196,384]{2,1,0:T(8,128)(2,1)} %images.1, bf16[12,196,384]{2,1,0:T(8,128)(2,1)} %cot.1, ...), custom_call_target="tpu_custom_call" | custom-call | tf_op jit(solution)/shard_map/pallas_call | solution.py:487
  187.1 0.0 all-reduce.2.cloned.1.call-update
  187.1 6.8 %bitcast_convert_fusion = (f32[1536,768]{1,0:T(8,128)}, f32[1536,768]{1,0:T(8,128)}) fusion(bf16[8,192,768]{2,1,0:T(8,128)(2,1)} %get-tuple-element.23, bf16[8,192,768]{2,1,0:T(8,128)(2,1)} %get-tuple-element.22), kind=kLoop, calls=%fused_computation | loop fusion | flops 2359296 | bytes 14155776 | tf_op jit(solution)/shard_map/convert_element_type | solution.py:571
  193.9 6.0 %copy.36 = f32[1536,768]{0,1:T(8,128)} copy(f32[1536,768]{1,0:T(8,128)} %get-tuple-element.33) | data formatting | bytes 9437184 | tf_op jit(solution)/shard_map/convert_element_type | solution.py:569
  200.0 3.7 %convert_element_type.22 = f32[12,196,384]{2,1,0:T(8,128)} convert(bf16[12,196,384]{2,1,0:T(8,128)(2,1)} %get-tuple-element.20) | non-fusion elementwise | flops 903168 | bytes 5419008 | tf_op jit(solution)/shard_map/convert_element_type | solution.py:560
  203.7 111.4 %all-reduce.2.cloned.1.call-done = f32[512,384]{1,0:T(8,128)} async-done(((f32[512,384]{1,0:T(8,128)}), f32[512,384]{1,0:T(8,128)}) %all-reduce.2.cloned.1.call-update) | async-done | bytes 786448 | tf_op jit(solution)/shard_map/psum | solution.py:554
  315.1 0.7 slice.44
  315.8 0.1 constant_dynamic-slice_fusion
  315.8 0.7 reshape.49
  316.5 1.9 slice_bitcast_fusion
  318.4 1.3 slice.43
  319.7 1.5 dynamic-slice_reduce_fusion
  321.2 0.0 copy-done
  321.2 1.2 copy.40
  (24 shorter events, 0.1 us)
Async XLA Ops:
  7.2 307.9 %all-reduce.2.cloned.1.call-start = ((), (), s32[]{:S(2)}) async-start(), calls=%async_computation | async-start | bytes 1572864 | tf_op jit(solution)/shard_map/psum | solution.py:554
  7.2 4.5 %copy-start.3 = (f32[384]{0:T(512)S(1)}, f32[384]{0:T(512)}, u32[]{:S(2)}) copy-start(f32[384]{0:T(512)} %param.20) | copy-start | bytes 4612
  7.2 5.3 %copy-start.1 = (bf16[384,196]{0,1:T(8,128)(2,1)S(1)}, bf16[384,196]{0,1:T(8,128)(2,1)}, u32[]{:S(2)}) copy-start(bf16[384,196]{0,1:T(8,128)(2,1)} %param.21) | copy-start | bytes 451588
  7.2 6.1 %copy-start.9 = (f32[196]{0:T(256)S(1)}, f32[196]{0:T(256)}, u32[]{:S(2)}) copy-start(f32[196]{0:T(256)} %param.22) | copy-start | bytes 2356
  7.3 6.8 %copy-start.4 = (f32[384]{0:T(512)S(1)}, f32[384]{0:T(512)}, u32[]{:S(2)}) copy-start(f32[384]{0:T(512)} %param.17) | copy-start | bytes 4612
  7.3 6.8 %copy-start.5 = (f32[384]{0:T(512)S(1)}, f32[384]{0:T(512)}, u32[]{:S(2)}) copy-start(f32[384]{0:T(512)} %param.18) | copy-start | bytes 4612
  7.3 6.8 %copy-start.6 = (f32[384]{0:T(512)S(1)}, f32[384]{0:T(512)}, u32[]{:S(2)}) copy-start(f32[384]{0:T(512)} %param.23) | copy-start | bytes 4612
  7.3 6.8 %copy-start.7 = (f32[384]{0:T(512)S(1)}, f32[384]{0:T(512)}, u32[]{:S(2)}) copy-start(f32[384]{0:T(512)} %param.24) | copy-start | bytes 4612
  7.3 6.9 %copy-start.8 = (f32[384]{0:T(512)S(1)}, f32[384]{0:T(512)}, u32[]{:S(2)}) copy-start(f32[384]{0:T(512)} %param.28) | copy-start | bytes 4612
  7.3 6.9 %copy-start.2 = (f32[1536]{0:T(1024)S(1)}, f32[1536]{0:T(1024)}, u32[]{:S(2)}) copy-start(f32[1536]{0:T(1024)} %param.26) | copy-start | bytes 18436
  200.0 121.2 %copy-start = (bf16[12,196,384]{2,1,0:T(8,128)(2,1)S(1)}, bf16[12,196,384]{2,1,0:T(8,128)(2,1)}, u32[]{:S(2)}) copy-start(bf16[12,196,384]{2,1,0:T(8,128)(2,1)} %get-tuple-element.48) | copy-start | bytes 5419012
Sparse Core Ops, SparseCore 0:
  187.2 127.7 all-reduce.1

commit v2 on v1

v2 whole, which is shorter than its diff:
```python
import functools

import jax
import jax.numpy as jnp
from jax import lax
from jax.experimental import pallas as pl
from jax.experimental.pallas import tpu as pltpu
from jax.sharding import PartitionSpec as P

MESH = pl.DeviceIdType.MESH
EPS = 1e-06
C0 = 0.7978845608028654
C1 = C0 * 0.044715
RING = 8
LOOK = 2
SOLO = 48
F32 = jnp.float32
BF16 = jnp.bfloat16


def dot(left, right, left_dim, right_dim):
    return lax.dot_general(
        left, right, (((left_dim,), (right_dim,)), ((), ())), preferred_element_type=F32
    )


def gelu(v):
    return v * (0.5 * jnp.tanh(v * (C0 + C1 * (v * v))) + 0.5)


def gelu_both(v):
    v2 = v * v
    h = 0.5 * jnp.tanh(v * (C0 + C1 * v2)) + 0.5
    return v * h, h + (h - h * h) * (v * (2 * C0 + 6 * C1 * v2))


def mod(v):
    return lax.rem(v + 2 * RING, RING)


def flip(index, step):
    return index + step - 2 * step * lax.rem(lax.div(index, step), 2)


def column(row, length):
    return jnp.transpose(jnp.broadcast_to(row.reshape(1, length), (8, length)))[:, 0:1]


def layer_kernel(
    groups,
    counts,
    images,
    cot,
    gain1,
    bias1,
    gain2,
    bias2,
    biasc,
    tw1,
    tb1,
    tw2,
    tb2,
    w1_own,
    w2_own,
    b1_own,
    out_o,
    gim_o,
    d2_o,
    d1_o,
    small_o,
    xh,
    xb,
    cb,
    ob,
    y2b,
    gb,
    res,
    acc,
    w1b,
    w2b,
    act,
    dg,
    stat,
    pb,
    bar,
    xr,
    rs,
    xs,
    vecb,
    b1h,
    b1v,
    t1v,
    t2v,
    vacc,
    small,
    small_c,
    small_x,
    small_s,
    small_r,
    loc_x,
    snd_x,
    rcv_x,
    loc_c,
    snd_c,
    rcv_c,
    loc_w,
    snd_w,
    rcv_w,
    snd_b,
    rcv_b,
    snd_h,
    rcv_h,
    snd_r,
    rcv_r,
    snd_e,
    rcv_e,
    snd_g,
    rcv_g,
    snd_f,
    rcv_f,
    loc_g,
    loc_o,
    snd_o,
    rcv_o,
    loc_i,
    snd_i,
    rcv_i,
    snd_s,
    rcv_s,
):
    imgs, patches, chans = xb.shape
    half = chans // 2
    pad = y2b.shape[0] // imgs
    piece = w2_own.shape[1]
    both = piece - 2 * SOLO
    keep_rows = SOLO + both
    dp, aa, ba = lax.axis_index("dp"), lax.axis_index("aa"), lax.axis_index("ba")
    lo, hi = lax.rem(dp, RING), lax.div(dp, RING)
    pos = jnp.where(lax.rem(lo, 2) == 0, lax.div(lo, 2), RING - 1 - lax.div(lo, 2))

    def at(place):
        place = mod(place)
        return hi * RING + jnp.where(
            place < RING // 2, 2 * place, 2 * (RING - 1 - place) + 1
        )

    dev_x = (dp, 1 - aa, ba)
    dev_c = (dp, aa, 1 - ba)
    dev_ring = ((at(pos + 1), aa, ba), (at(pos - 1), aa, ba))
    dev_fly = []
    step = 1
    while step < RING * groups:
        dev_fly.append((flip(dp, step), aa, ba))
        step *= 2
    dev_hi = dev_fly[3:]
    peers = [dev_x, dev_c, *dev_ring, *dev_fly]
    barrier = pltpu.get_barrier_semaphore()
    for peer in peers:
        pl.semaphore_signal(barrier, inc=1, device_id=peer, device_id_type=MESH)

    mine = pl.ds(pl.multiple_of(aa * half, half), half)
    other = pl.ds(pl.multiple_of((1 - aa) * half, half), half)
    rows_mine = pl.ds(pl.multiple_of(ba * piece, 64), piece)
    rows_other = pl.ds(pl.multiple_of((1 - ba) * piece, 64), piece)

    def remote(src, dst, send, recv, dev):
        return pltpu.make_async_remote_copy(
            src_ref=src,
            dst_ref=dst,
            send_sem=send,
            recv_sem=recv,
            device_id=dev,
            device_id_type=MESH,
        )

    def local_in(src, dst, sem, i):
        return pltpu.make_async_copy(src.at[aa * imgs + i], dst.at[i, :, mine], sem.at[i])

    def give(src, dst, send, recv, i):
        return remote(
            src.at[(1 - aa) * imgs + i], dst.at[i, :, mine], send.at[i], recv.at[i], dev_x
        )

    def take(src, dst, send, recv, i):
        return remote(
            src.at[(1 - aa) * imgs + i], dst.at[i, :, other], send.at[i], recv.at[i], dev_x
        )

    cols = 2 * piece
    parts = w1_own.shape[1] // cols

    def w1_in(k):
        return pltpu.make_async_copy(
            w1_own.at[:, pl.ds(k * cols, cols)], act.at[k, pl.ds(0, chans), :], loc_w.at[1 + k]
        )

    for k in range(parts):
        w1_in(k).start()
    for i in range(imgs):
        local_in(images, xb, loc_x, i).start()
    w2_local = pltpu.make_async_copy(w2_own, w2b.at[:, rows_mine, :], loc_w.at[0])
    w2_local.start()
    for i in range(imgs):
        local_in(cot, cb, loc_c, i).start()
    for k, ref in enumerate((gain1, bias1, gain2, bias2, biasc)):
        vecb[aa, k : k + 1, :] = ref[...].reshape(1, half)
    b1h[ba] = b1_own[...].reshape(1, parts * cols)

    pl.semaphore_wait(barrier, len(peers))

    vec_copy = remote(vecb.at[aa], vecb.at[aa], snd_w.at[2], rcv_w.at[2], dev_x)
    vec_copy.start()
    for i in range(LOOK):
        give(images, xb, snd_x, rcv_x, i).start()
    b1_copy = remote(b1h.at[ba], b1h.at[ba], snd_w.at[3], rcv_w.at[3], dev_c)
    b1_copy.start()
    w2_copy = remote(w2_own, w2b.at[:, rows_mine, :], snd_w.at[0], rcv_w.at[0], dev_c)
    w2_copy.start()
    y2b[...] = jnp.zeros(y2b.shape, BF16)
    gb[...] = jnp.zeros(gb.shape, BF16)
    rs[0] = jnp.zeros(rs.shape[1:], BF16)
    vacc[...] = jnp.zeros(vacc.shape, F32)
    small[...] = jnp.zeros(small.shape, F32)
    t1v[...] = column(tb1[...], t1v.shape[0])
    t2v[...] = column(tb2[...], patches)
    for k in range(parts):
        w1_in(k).wait()
        turned = jnp.transpose(act[k, 0:chans, :])
        w1b[2 * k, rows_mine, :] = turned[:piece]
        w1b[2 * k + 1, rows_mine, :] = turned[piece:]
    w1_copy = remote(
        w1b.at[:, rows_mine, :], w1b.at[:, rows_mine, :], snd_w.at[1], rcv_w.at[1], dev_c
    )
    w1_copy.start()
    vec_copy.wait_send()
    remote(vecb.at[aa], vecb.at[1 - aa], snd_w.at[2], rcv_w.at[2], dev_x).wait_recv()
    b1_copy.wait_send()
    remote(b1h.at[ba], b1h.at[1 - ba], snd_w.at[3], rcv_w.at[3], dev_c).wait_recv()
    for q in range(RING):
        b1v[q : q + 1, :] = jnp.concatenate(
            [b1h[0, :, q * piece : (q + 1) * piece], b1h[1, :, q * piece : (q + 1) * piece]],
            axis=1,
        )

    def vec(k):
        return jnp.concatenate([vecb[0, k : k + 1, :], vecb[1, k : k + 1, :]], axis=1)

    def token_forward(i):
        local_in(images, xb, loc_x, i).wait()
        take(images, xb, snd_x, rcv_x, i).wait()

        @pl.when(i + LOOK < imgs)
        def _():
            give(images, xb, snd_x, rcv_x, i + LOOK).start()

        @pl.when(i + LOOK >= imgs)
        def _():
            give(cot, cb, snd_c, rcv_c, i + LOOK - imgs).start()

        x = xb[i].astype(F32)
        mean = jnp.mean(x, -1, keepdims=True)
        xc = x - mean
        rstd = lax.rsqrt(jnp.mean(xc * xc, -1, keepdims=True) + EPS)
        stat[i, :, 0 : 1] = mean
        stat[i, :, 1 : 2] = rstd
        y1 = (xc * rstd * vec(0) + vec(1)).astype(BF16)
        hid = gelu(dot(tw1[...], y1, 0, 0) + t1v[...]).astype(BF16)
        row = x + dot(tw2[...], hid, 1, 0) + t2v[...]
        res[i] = row
        mean = jnp.mean(row, -1, keepdims=True)
        xc = row - mean
        rstd = lax.rsqrt(jnp.mean(xc * xc, -1, keepdims=True) + EPS)
        stat[i, :, 2 : 3] = mean
        stat[i, :, 3 : 4] = rstd
        y2 = (xc * rstd * vec(2) + vec(3)).astype(BF16)
        y2b[pl.ds(pl.multiple_of(i * pad, 16), patches), :] = y2

    def weight(i):
        return jnp.where(aa * imgs + i < counts[0], 1.0, 0.0).astype(F32)

    chunks = 3
    size = y2b.shape[0] // chunks
    each = imgs // chunks

    def chan_forward(chunk, pair):
        rows = pl.ds(pl.multiple_of(chunk * size, 16), size)
        win = w1b[pl.ds(2 * pair, 2)].reshape(2 * cols, chans)
        wout = w2b[pl.ds(2 * pair, 2)].reshape(2 * cols, chans)
        bias = jnp.concatenate(
            [b1v[pl.ds(2 * pair, 1), :], b1v[pl.ds(2 * pair + 1, 1), :]], axis=1
        )
        val, der = gelu_both(dot(y2b[rows, :], win, 1, 1) + bias)
        val = val.astype(BF16)
        der = der.astype(BF16)
        act[2 * pair, rows, :] = val[:, :cols]
        act[2 * pair + 1, rows, :] = val[:, cols:]
        dg[2 * pair, rows, :] = der[:, :cols]
        dg[2 * pair + 1, rows, :] = der[:, cols:]
        new = dot(val, wout, 1, 0)
        acc[rows, :] = jnp.where(pair == 0, 0.0, acc[rows, :]) + new

    def forward_chunk(chunk, carry):
        def one(k, carry):
            token_forward(chunk * each + k)
            return carry

        lax.fori_loop(0, each, one, 0)

        @pl.when(chunk == 0)
        def _():
            w2_local.wait()
            w2_copy.wait_send()
            remote(
                w2_own, w2b.at[:, rows_other, :], snd_w.at[0], rcv_w.at[0], dev_c
            ).wait_recv()
            w1_copy.wait_send()
            remote(
                w1b.at[:, rows_mine, :], w1b.at[:, rows_other, :], snd_w.at[1], rcv_w.at[1], dev_c
            ).wait_recv()

        def two(k, carry):
            chan_forward(chunk, k)
            return carry

        lax.fori_loop(0, RING // 2, two, 0)

        def three(k, carry):
            i = chunk * each + k
            rows = pl.ds(pl.multiple_of(i * pad, 16), patches)
            ob[i] = (weight(i) * (res[i] + acc[rows, :] + vec(4))).astype(BF16)
            return carry

        lax.fori_loop(0, each, three, 0)
        return carry

    lax.fori_loop(0, chunks, forward_chunk, 0)
    for i in range(LOOK, imgs):
        give(cot, cb, snd_c, rcv_c, i).start()

    def mask_cot(i, carry):
        local_in(cot, cb, loc_c, i).wait()
        take(cot, cb, snd_c, rcv_c, i).wait()
        rows = pl.ds(pl.multiple_of(i * pad, 16), patches)
        gb[rows, :] = (cb[i].astype(F32) * weight(i)).astype(BF16)
        return carry

    lax.fori_loop(0, imgs, mask_cot, 0)

    def out_local(i):
        return pltpu.make_async_copy(ob.at[i, :, mine], out_o.at[aa * imgs + i], loc_o.at[i])

    def out_remote(i, sender):
        return remote(
            ob.at[i, :, other], out_o.at[sender * imgs + i], snd_o.at[i], rcv_o.at[i], dev_x
        )

    def grad_local(i):
        return pltpu.make_async_copy(xb.at[i, :, mine], gim_o.at[aa * imgs + i], loc_i.at[i])

    def grad_remote(i, sender):
        return remote(
            xb.at[i, :, other], gim_o.at[sender * imgs + i], snd_i.at[i], rcv_i.at[i], dev_x
        )

    ones = jnp.ones((8, chans), BF16)

    def token_backward(i):
        rows = pl.ds(pl.multiple_of(i * pad, 16), patches)
        up = acc[rows, :]
        grad_out = gb[rows, :].astype(F32)
        rstd = stat[i, :, 3 : 4]
        normed = (res[i] - stat[i, :, 2 : 3]) * rstd
        vacc[2:3, :] += jnp.sum(up * normed, 0, keepdims=True)
        vacc[3:4, :] += jnp.sum(up, 0, keepdims=True)
        vacc[4:5, :] += jnp.sum(grad_out, 0, keepdims=True)
        q = up * vec(2)
        mean = jnp.mean(q, -1, keepdims=True)
        proj = jnp.mean(q * normed, -1, keepdims=True)
        grad_res = grad_out + rstd * (q - mean - normed * proj)
        grad_tok = grad_res.astype(BF16)
        rstd = stat[i, :, 1 : 2]
        normed = (xb[i].astype(F32) - stat[i, :, 0 : 1]) * rstd
        y1 = (normed * vec(0) + vec(1)).astype(BF16)
        val, der = gelu_both(dot(tw1[...], y1, 0, 0) + t1v[...])
        small[200 : 200 + patches, :] += dot(grad_tok, val.astype(BF16), 1, 1)
        small[408:416, 0:patches] += dot(ones, grad_tok, 1, 1)
        grad_pre = (dot(tw2[...], grad_tok, 0, 0) * der).astype(BF16)
        small[0:patches, :] += dot(y1, grad_pre, 1, 1)
        small[400:408, :] += dot(ones, grad_pre, 1, 1)
        up = dot(tw1[...], grad_pre, 1, 0)
        vacc[0:1, :] += jnp.sum(up * normed, 0, keepdims=True)
        vacc[1:2, :] += jnp.sum(up, 0, keepdims=True)
        q = up * vec(0)
        mean = jnp.mean(q, -1, keepdims=True)
        proj = jnp.mean(q * normed, -1, keepdims=True)
        xb[i] = (grad_res + rstd * (q - mean - normed * proj)).astype(BF16)
        grad_local(i).start()
        grad_remote(i, aa).start()

    bars = bar.shape[0]
    solo_mine = pl.ds(pl.multiple_of(aa * SOLO, 16), SOLO)
    solo_other = pl.ds(pl.multiple_of((1 - aa) * SOLO, 16), SOLO)
    shared = pl.ds(2 * SOLO, both)

    def own_rows(place, size):
        return pl.ds(pl.multiple_of(ba * piece + place, 16), size)

    def to_core(s, a):
        return remote(
            pb.at[lax.rem(s, 2), a, rows_other, :],
            bar.at[lax.rem(s, bars), a],
            snd_b.at[lax.rem(s, bars), a],
            rcv_b.at[lax.rem(s, bars), a],
            dev_c,
        )

    def to_x(s, a):
        return remote(
            bar.at[lax.rem(s, bars), a, solo_other, :],
            xr.at[lax.rem(s, 2), a],
            snd_h.at[lax.rem(s, 2), a],
            rcv_h.at[lax.rem(s, 2), a],
            dev_x,
        )

    ring_rows = (pl.ds(0, SOLO), pl.ds(SOLO, both))

    def to_ring(s, a, c):
        return remote(
            rs.at[s, a, ring_rows[c], :],
            rs.at[s + 1, a, ring_rows[c], :],
            snd_r.at[s, a, c],
            rcv_r.at[s, a, c],
            dev_ring[a],
        )

    def first_sum(s, a):
        to_core(s, a).wait_recv()
        slot = lax.rem(s, bars)
        own = own_rows((1 - aa) * SOLO, SOLO)
        total = pb[lax.rem(s, 2), a, own, :].astype(F32) + bar[slot, a, solo_other, :].astype(F32)
        bar[slot, a, solo_other, :] = total.astype(BF16)
        to_x(s, a).start()

    def second_sum(s, a):
        par = lax.rem(s, 2)
        slot = lax.rem(s, bars)
        for c in (1, 0):
            if c == 0:
                to_x(s, a).wait()

            @pl.when(s > 0)
            def _():
                to_ring(s - 1, a, c).wait_recv()

            if c == 0:
                more = (
                    pb[par, a, own_rows(aa * SOLO, SOLO), :].astype(F32)
                    + bar[slot, a, solo_mine, :].astype(F32)
                    + xr[par, a].astype(F32)
                )
            else:
                more = pb[par, a, own_rows(2 * SOLO, both), :].astype(F32) + bar[
                    slot, a, shared, :
                ].astype(F32)
            rs[s, a, ring_rows[c], :] = (rs[s, a, ring_rows[c], :].astype(F32) + more).astype(BF16)

            @pl.when(s < RING - 1)
            def _():
                to_ring(s, a, c).start()

    def chan_backward(j, carry):
        @pl.when(j < RING)
        def _():
            par = lax.rem(j, 2)

            @pl.when(j >= 2)
            def _():
                for a in range(2):
                    to_core(j - 2, a).wait_send()

            pb[par, 0] = dot(act[mod(pos - 1 - j)], gb[...], 0, 0).astype(BF16)
            to_core(j, 0).start()

        @pl.when(j > 0)
        def _():
            for a in range(2):
                first_sum(j - 1, a)

        @pl.when(j < RING)
        def _():
            left = mod(pos + 1 + j)
            grad = (dot(gb[...], w2b[left], 1, 1) * dg[left].astype(F32)).astype(BF16)
            small[pl.ds(416 + left, 1), :] = jnp.sum(grad.astype(F32), 0, keepdims=True)
            pb[lax.rem(j, 2), 1] = dot(grad, y2b[...], 0, 0).astype(BF16)
            to_core(j, 1).start()
            acc[...] = jnp.where(j == 0, 0.0, acc[...]) + dot(grad, w1b[left], 1, 0)

        @pl.when(j == RING)
        def _():
            token_backward(0)

        @pl.when(j > 0)
        def _():
            for a in range(2):
                second_sum(j - 1, a)

        @pl.when(j < imgs)
        def _():
            out_local(j).start()
            out_remote(j, aa).start()

        return carry

    lax.fori_loop(0, RING + 1, chan_backward, 0)
    for s in (RING - 2, RING - 1):
        for a in range(2):
            to_core(s, a).wait_send()

    last = RING - 1
    results = (d2_o, d1_o)
    gather_rows = (solo_mine, shared)

    def gather(t, a, c, src):
        q = mod(pos - t) if a == 0 else mod(pos + t)
        dst = results[a].at[q, gather_rows[c], :]
        return remote(
            dst if src is None else src, dst, snd_g.at[t, a, c], rcv_g.at[t, a, c], dev_ring[a]
        )

    def gather_arrival(t, a, c):
        q = mod(pos - 1 - t) if a == 0 else mod(pos + 1 + t)
        dst = results[a].at[q, gather_rows[c], :]
        return remote(dst, dst, snd_g.at[t, a, c], rcv_g.at[t, a, c], dev_ring[a])

    def across(t, a, src):
        q = mod(pos - t) if a == 0 else mod(pos + t)
        dst = results[a].at[q, solo_mine, :]
        return remote(dst if src is None else src, dst, snd_f.at[t, a], rcv_f.at[t, a], dev_x)

    def across_arrival(t, a):
        q = mod(pos - t) if a == 0 else mod(pos + t)
        dst = results[a].at[q, solo_other, :]
        return remote(dst, dst, snd_f.at[t, a], rcv_f.at[t, a], dev_x)

    def add_hi(c):
        for k, dev in enumerate(dev_hi):
            for a in range(2):
                src = rs.at[last, a, ring_rows[c], :]
                landed = xh.at[k, a, ring_rows[c], :]
                near = pb.at[0, 0, ring_rows[c], :]
                copy = remote(src, landed, snd_e.at[1 + k, a, c], rcv_e.at[1 + k, a, c], dev)
                copy.start()
                copy.wait()
                back = pltpu.make_async_copy(landed, near, loc_g.at[a, c])
                back.start()
                back.wait()
                rs[last, a, ring_rows[c], :] = (
                    rs[last, a, ring_rows[c], :].astype(F32) + pb[0, 0, ring_rows[c], :].astype(F32)
                ).astype(BF16)

    keep = []

    def start_gather(c):
        add_hi(c)
        for a in range(2):
            src = rs.at[last, a, ring_rows[c], :]
            gather(0, a, c, src).start()
            if c == 0:
                across(0, a, src).start()
            keep.append(
                pltpu.make_async_copy(
                    src, results[a].at[pos, gather_rows[c], :], loc_g.at[a, c]
                )
            )
            keep[-1].start()

    swaps = [
        remote(rs.at[last, a, ring_rows[1], :], xs.at[a], snd_e.at[0, a, 1], rcv_e.at[0, a, 1], dev_x)
        for a in range(2)
    ]
    for copy in swaps:
        copy.start()
    start_gather(0)
    token_backward(1)
    for a, copy in enumerate(swaps):
        copy.wait()
        total = rs[last, a, ring_rows[1], :].astype(F32) + xs[a].astype(F32)
        rs[last, a, ring_rows[1], :] = total.astype(BF16)
    start_gather(1)

    def pass_on(t):
        for c in range(2):
            for a in range(2):
                gather_arrival(t, a, c).wait_recv()

                @pl.when(t + 1 < RING - 1)
                def _():
                    gather(t + 1, a, c, None).start()

                if c == 0:
                    across(t + 1, a, None).start()

    def token_and_gather(t, carry):
        token_backward(t + 2)
        pass_on(t)
        return carry

    lax.fori_loop(0, imgs - 2, token_and_gather, 0)
    small[424:432, :] = vacc[:, :half]
    small[432:440, :] = vacc[:, half:]

    total_rows = small.shape[0]
    half_rows, quarter = total_rows // 2, total_rows // 4
    own_half = pl.ds(pl.multiple_of(ba * half_rows, 256), half_rows)
    other_half = pl.ds(pl.multiple_of((1 - ba) * half_rows, 256), half_rows)
    own_quarter = pl.ds(pl.multiple_of(ba * half_rows + aa * quarter, 128), quarter)
    other_quarter = pl.ds(pl.multiple_of(ba * half_rows + (1 - aa) * quarter, 128), quarter)
    flies = len(dev_fly)

    small_steps = [
        remote(small.at[other_half, :], small_c, snd_s.at[0], rcv_s.at[0], dev_c),
        remote(small.at[other_quarter, :], small_x, snd_s.at[1], rcv_s.at[1], dev_x),
    ]
    for k, dev in enumerate(dev_fly):
        small_steps.append(
            remote(small_s.at[k], small_r.at[k], snd_s.at[2 + k], rcv_s.at[2 + k], dev)
        )
    for k, (rows, dev) in enumerate(((own_quarter, dev_x), (own_half, dev_c))):
        region = small_o.at[rows, :]
        n = 2 + flies + k
        small_steps.append(remote(region, region, snd_s.at[n], rcv_s.at[n], dev))

    def small_start(n):
        if n == 2:
            small_s[0] = small[own_quarter, :].astype(BF16)
        small_steps[n].start()

    def small_finish(n):
        if n < 2 + flies:
            small_steps[n].wait()
        if n == 0:
            small[own_half, :] += small_c[...]
        elif n == 1:
            small[own_quarter, :] += small_x[...]
        elif n < 2 + flies:
            total = small_s[n - 2].astype(F32) + small_r[n - 2].astype(F32)
            if n + 1 < 2 + flies:
                small_s[n - 1] = total.astype(BF16)
            else:
                small_o[own_quarter, :] = total.astype(BF16)
        else:
            rows = other_quarter if n == 2 + flies else other_half
            region = small_o.at[rows, :]
            small_steps[n].wait_send()
            remote(region, region, snd_s.at[n], rcv_s.at[n], dev_x).wait_recv()

    small_start(0)
    done = 0
    for t in range(imgs - 2, RING - 1):
        pass_on(t)
        small_finish(done)
        done += 1
        small_start(done)
    while done < len(small_steps):
        small_finish(done)
        done += 1
        if done < len(small_steps):
            small_start(done)

    for copy in keep:
        copy.wait()

    def drain_images(i, carry):
        out_local(i).wait()
        out_remote(i, 1 - aa).wait()
        grad_local(i).wait()
        grad_remote(i, 1 - aa).wait()
        return carry

    lax.fori_loop(0, imgs, drain_images, 0)

    def drain_ring(t, carry):
        for a in range(2):
            across_arrival(t, a).wait()

            @pl.when(t < RING - 1)
            def _():
                for c in range(2):
                    to_ring(t, a, c).wait_send()
                    gather_arrival(t, a, c).wait_send()

        return carry

    lax.fori_loop(0, RING, drain_ring, 0)


def finish_kernel(gim, d2, d1, small, gim_o, w2_o, w1_o, tw1_o, tw2_o, tb1_o, tb2_o, b1_o, *vec_o):
    count, piece, chans = d1.shape
    gim_o[...] = gim[...].astype(F32)
    w2_o[...] = d2[...].reshape(count * piece, chans).astype(F32)
    w1_o[...] = jnp.transpose(d1[...].reshape(count * piece, chans)).astype(F32)

    @pl.when(pl.program_id(0) == 0)
    def _():
        aa, ba = lax.axis_index("aa"), lax.axis_index("ba")
        patches = tw1_o.shape[0]
        tw1_o[...] = small[0:patches, :].astype(F32)
        tw2_o[...] = small[200 : 200 + patches, :].astype(F32)
        tb1_o[...] = small[400:401, :].astype(F32).reshape(tb1_o.shape)
        tb2_o[...] = small[408:409, 0:patches].astype(F32).reshape(patches)
        rows = small[416:424, :].astype(F32)
        rows = jnp.where(ba == 0, rows[:, :piece], rows[:, piece:])
        rows = jnp.concatenate([rows[q : q + 1, :] for q in range(RING)], axis=1)
        b1_o[...] = rows.reshape(b1_o.shape)
        rows = jnp.where(aa == 0, small[424:432, :].astype(F32), small[432:440, :].astype(F32))
        for k, ref in enumerate(vec_o):
            ref[...] = rows[k : k + 1, :].reshape(ref.shape)


def local(groups, images, counts, ln1_gain, ln1_bias, tok_w1, tok_b1, tok_w2, tok_b2,
          ln2_gain, ln2_bias, ch_w1, ch_b1, ch_w2, ch_b2, cotangent):
    slots, patches, half = images.shape
    chans = 2 * half
    imgs = slots // 2
    pad = -(-patches // 16) * 16
    hidden = ch_w1.shape[1]
    piece = hidden // RING
    both = piece - 2 * SOLO
    keep_rows = SOLO + both
    hid_tok = tok_w1.shape[1]
    total = 512
    flies = 3
    while RING * groups > 2**flies:
        flies += 1
    his = max(flies - 3, 1)
    vmem = pl.BlockSpec(memory_space=pltpu.VMEM)
    hbm = pl.BlockSpec(memory_space=pl.ANY)
    dma = pltpu.SemaphoreType.DMA
    per_image = [dma((imgs,))] * 3
    out, gim, d2, d1, small, _ = pl.pallas_call(
        functools.partial(layer_kernel, groups),
        out_shape=[
            jax.ShapeDtypeStruct((slots, patches, half), BF16),
            jax.ShapeDtypeStruct((slots, patches, half), BF16),
            jax.ShapeDtypeStruct((RING, piece, chans), BF16),
            jax.ShapeDtypeStruct((RING, piece, chans), BF16),
            jax.ShapeDtypeStruct((total, hid_tok), BF16),
            jax.ShapeDtypeStruct((his, 2, keep_rows if groups > 1 else 16, chans), BF16),
        ],
        in_specs=[pl.BlockSpec(memory_space=pltpu.SMEM), hbm, hbm]
        + [vmem] * 9
        + [hbm] * 2
        + [vmem],
        out_specs=[hbm] * 4 + [vmem, hbm],
        scratch_shapes=[
            pltpu.VMEM((imgs, patches, chans), BF16),
            pltpu.VMEM((imgs, patches, chans), BF16),
            pltpu.VMEM((imgs, patches, chans), BF16),
            pltpu.VMEM((imgs * pad, chans), BF16),
            pltpu.VMEM((imgs * pad, chans), BF16),
            pltpu.VMEM((imgs, patches, chans), F32),
            pltpu.VMEM((imgs * pad, chans), F32),
            pltpu.VMEM((RING, 2 * piece, chans), BF16),
            pltpu.VMEM((RING, 2 * piece, chans), BF16),
            pltpu.VMEM((RING, imgs * pad, 2 * piece), BF16),
            pltpu.VMEM((RING, imgs * pad, 2 * piece), BF16),
            pltpu.VMEM((imgs, patches, 4), F32),
            pltpu.VMEM((2, 2, 2 * piece, chans), BF16),
            pltpu.VMEM((4, 2, piece, chans), BF16),
            pltpu.VMEM((2, 2, SOLO, chans), BF16),
            pltpu.VMEM((RING, 2, keep_rows, chans), BF16),
            pltpu.VMEM((2, both, chans), BF16),
            pltpu.VMEM((2, 8, half), F32),
            pltpu.VMEM((2, 1, hidden), F32),
            pltpu.VMEM((RING, 2 * piece), F32),
            pltpu.VMEM((hid_tok, 1), F32),
            pltpu.VMEM((patches, 1), F32),
            pltpu.VMEM((8, chans), F32),
            pltpu.VMEM((total, hid_tok), F32),
            pltpu.VMEM((total // 2, hid_tok), F32),
            pltpu.VMEM((total // 4, hid_tok), F32),
            pltpu.VMEM((flies, total // 4, hid_tok), BF16),
            pltpu.VMEM((flies, total // 4, hid_tok), BF16),
            *per_image,
            *per_image,
            dma((5,)),
            dma((4,)),
            dma((4,)),
            dma((4, 2)),
            dma((4, 2)),
            dma((2, 2)),
            dma((2, 2)),
            dma((RING, 2, 2)),
            dma((RING, 2, 2)),
            dma((1 + his, 2, 2)),
            dma((1 + his, 2, 2)),
            dma((RING, 2, 2)),
            dma((RING, 2, 2)),
            dma((RING, 2)),
            dma((RING, 2)),
            dma((2, 2)),
            *per_image,
            *per_image,
            dma((4 + flies,)),
            dma((4 + flies,)),
        ],
        compiler_params=pltpu.CompilerParams(
            collective_id=0, has_side_effects=True, vmem_limit_bytes=65100 * 1024
        ),
    )(
        counts,
        images,
        cotangent,
        ln1_gain,
        ln1_bias,
        ln2_gain,
        ln2_bias,
        ch_b2,
        tok_w1,
        tok_b1,
        tok_w2.T,
        tok_b2,
        ch_w1,
        ch_w2.reshape(RING, piece, chans),
        ch_b1,
    )
    steps = RING // 2
    row = jax.ShapeDtypeStruct((half,), F32)

    def whole(*shape):
        return pl.BlockSpec(shape, lambda k: (0,) * len(shape))

    some = pl.BlockSpec((slots // steps, patches, half), lambda k: (k, 0, 0))
    pair = pl.BlockSpec((2, piece, chans), lambda k: (k, 0, 0))
    gim, w2, w1, tw1, tw2, tb1, tb2, b1, g1, n1, g2, n2, c2 = pl.pallas_call(
        finish_kernel,
        grid=(steps,),
        out_shape=[
            jax.ShapeDtypeStruct((slots, patches, half), F32),
            jax.ShapeDtypeStruct((hidden, chans), F32),
            jax.ShapeDtypeStruct((chans, hidden), F32),
            jax.ShapeDtypeStruct((patches, hid_tok), F32),
            jax.ShapeDtypeStruct((patches, hid_tok), F32),
            jax.ShapeDtypeStruct((hid_tok,), F32),
            jax.ShapeDtypeStruct((patches,), F32),
            jax.ShapeDtypeStruct((hidden,), F32),
        ]
        + [row] * 5,
        in_specs=[some, pair, pair, whole(total, hid_tok)],
        out_specs=[
            some,
            pl.BlockSpec((2 * piece, chans), lambda k: (k, 0)),
            pl.BlockSpec((chans, 2 * piece), lambda k: (0, k)),
            whole(patches, hid_tok),
            whole(patches, hid_tok),
            whole(hid_tok),
            whole(patches),
            whole(hidden),
        ]
        + [whole(half)] * 5,
        compiler_params=pltpu.CompilerParams(vmem_limit_bytes=62 * 2**20),
    )(gim, d2, d1, small)
    return out, gim, g1, n1, tw1, tb1, tw2.T, tb2, g2, n2, w1, b1, w2, c2


def solution(mesh):
    rows = P(("dp", "ba"), None, "aa")
    chan = P("aa")
    placed = (rows, P(("dp", "ba")), chan, chan, P(), P(), P(), P(), chan, chan,
              P(None, "ba"), P("ba"), P("ba", None), chan, rows)
    given = (rows, rows, chan, chan, P(), P(), P(), P(), chan, chan,
             P(None, "ba"), P("ba"), P("ba", None), chan)
    return jax.shard_map(
        functools.partial(local, mesh.shape["dp"] // RING),
        mesh=mesh,
        in_specs=placed,
        out_specs=given,
        check_vma=False,
    )
```

time: 330 us -> 199 us (0.60)
  waiting for transfers between devices: 111 us -> 0 us
  Pallas kernels: 170 us -> 196 us
  local copies, waits for them, and re-layouts: 21.5 us -> 1.24 us
  between operations: 14.8 us -> 1.33 us
  other arithmetic: 11 us -> 0 us
    psum x1 -> x0, waiting for transfers between devices: 111 us -> none  [local(): small = lax.psum(small, ('dp', 'aa', 'ba'))]
    pallas_call x1, Pallas kernels: 170 us -> 187 us  [local(): pl.pallas_call(functools.partial(layer_kernel, groups), out_shape=[jax.Sh...]
    convert_element_type x3 -> x0, other arithmetic: 11 us -> none  [the longest x1 6.79 us: local(): d2.reshape(hidden, chans).astype(F32)]
    pallas_call x0 -> x1, Pallas kernels: none -> 8.8 us  [local(): pl.pallas_call(finish_kernel, grid=(steps,), out_shape=[jax.ShapeDtypeStr...]
    transpose x2 -> x0, local copies, waits for them, and re-layouts: 6.29 us -> none  [the longest x1 4.38 us: local(): w1 = ch_w1.T.reshape(RING, piece, chans)]
    convert_element_type x1 -> x0, local copies, waits for them, and re-layouts: 6.05 us -> none  [local(): d1.reshape(hidden, chans).T.astype(F32)]
    slice x3 -> x0, local copies, waits for them, and re-layouts: 3.49 us -> none  [the longest x1 1.52 us: local(): rows[4]]
  transfers between devices with their start and end apart: 1 -> 0, of which waited for: 1 -> 0; matrix products, arithmetic and copies ran while one was open for 5% -> 0% of each run, Pallas kernels for 0% -> 0%
where the time goes in v2:
time: 199 us; the launch traced here: 198 us
  Pallas kernels  196 us (98%)
    pallas_call x1, Pallas kernels, local(): pl.pallas_call(functools.partial(layer_kernel, groups), out_shape=[jax.Sh...  187 us
    pallas_call x1, Pallas kernels, local(): pl.pallas_call(finish_kernel, grid=(steps,), out_shape=[jax.ShapeDtypeStr...  8.8 us

profile of v2, /device:TPU:0, one launch (start us, length us, event | category | flops | bytes accessed | tf_op | source)
XLA Modules:
  0.0 198.3 jit_solution(1851542732094270960)
XLA Ops:
  1.3 186.9 %shard_map.254 = (bf16[12,196,384]{2,1,0:T(8,128)(2,1)}, bf16[12,196,384]{2,1,0:T(8,128)(2,1)}, bf16[8,192,768]{2,1,0:T(8,128)(2,1)}, bf16[8,192,768]{2,1,0:T(8,...) custom-call(s32[1]{0:T(128)S(6)} %copy.30.counts, bf16[12,196,384]{2,1,0:T(8,128)(2,1)} %images.1, ...), custom_call_target="tpu_custom_call" | custom-call | tf_op jit(solution)/shard_map/pallas_call | solution.py:741
  188.2 0.0 copy-start
  188.3 8.8 %shard_map.255 = (f32[12,196,384]{2,1,0:T(8,128)}, f32[1536,768]{1,0:T(8,128)}, f32[768,1536]{1,0:T(8,128)}, f32[196,384]{1,0:T(8,128)}, f32[196,384]{1,0:T(8,12...) custom-call(bf16[12,196,384]{2,1,0:T(8,128)(2,1)} %get-tuple-element, ...), custom_call_target="tpu_custom_call" | custom-call | tf_op jit(solution)/shard_map/pallas_call | solution.py:836
  197.1 0.0 copy-done
  197.1 1.2 copy.31
Async XLA Ops:
  188.2 8.8 %copy-start = (bf16[12,196,384]{2,1,0:T(8,128)(2,1)S(1)}, bf16[12,196,384]{2,1,0:T(8,128)(2,1)}, u32[]{:S(2)}) copy-start(bf16[12,196,384]{2,1,0:T(8,128)(2,1)} %get-tuple-element.64) | copy-start | bytes 5419012

commit v3 on v2

--- a/solution.py
+++ b/solution.py
@@ -12,8 +12,8 @@
 C0 = 0.7978845608028654
 C1 = C0 * 0.044715
 RING = 8
-LOOK = 2
-SOLO = 48
+LOOK = 3
+SOLO = 32
 F32 = jnp.float32
 BF16 = jnp.bfloat16
 
@@ -71,7 +71,6 @@
     xh,
     xb,
     cb,
-    ob,
     y2b,
     gb,
     res,
@@ -84,8 +83,10 @@
     pb,
     bar,
     xr,
+    held,
     rs,
     xs,
+    fs,
     vecb,
     b1h,
     b1v,
@@ -116,8 +117,6 @@
     rcv_e,
     snd_g,
     rcv_g,
-    snd_f,
-    rcv_f,
     loc_g,
     loc_o,
     snd_o,
@@ -128,12 +127,11 @@
     snd_s,
     rcv_s,
 ):
-    imgs, patches, chans = xb.shape
-    half = chans // 2
+    _, imgs, patches, half = xb.shape
+    chans = 2 * half
     pad = y2b.shape[0] // imgs
     piece = w2_own.shape[1]
     both = piece - 2 * SOLO
-    keep_rows = SOLO + both
     dp, aa, ba = lax.axis_index("dp"), lax.axis_index("aa"), lax.axis_index("ba")
     lo, hi = lax.rem(dp, RING), lax.div(dp, RING)
     pos = jnp.where(lax.rem(lo, 2) == 0, lax.div(lo, 2), RING - 1 - lax.div(lo, 2))
@@ -158,8 +156,6 @@
     for peer in peers:
         pl.semaphore_signal(barrier, inc=1, device_id=peer, device_id_type=MESH)
 
-    mine = pl.ds(pl.multiple_of(aa * half, half), half)
-    other = pl.ds(pl.multiple_of((1 - aa) * half, half), half)
     rows_mine = pl.ds(pl.multiple_of(ba * piece, 64), piece)
     rows_other = pl.ds(pl.multiple_of((1 - ba) * piece, 64), piece)
 
@@ -174,17 +170,25 @@
         )
 
     def local_in(src, dst, sem, i):
-        return pltpu.make_async_copy(src.at[aa * imgs + i], dst.at[i, :, mine], sem.at[i])
+        return pltpu.make_async_copy(src.at[aa * imgs + i], dst.at[aa, i], sem.at[i])
 
     def give(src, dst, send, recv, i):
         return remote(
-            src.at[(1 - aa) * imgs + i], dst.at[i, :, mine], send.at[i], recv.at[i], dev_x
+            src.at[(1 - aa) * imgs + i], dst.at[aa, i], send.at[i], recv.at[i], dev_x
         )
 
     def take(src, dst, send, recv, i):
         return remote(
-            src.at[(1 - aa) * imgs + i], dst.at[i, :, other], send.at[i], recv.at[i], dev_x
-        )
+            src.at[(1 - aa) * imgs + i], dst.at[1 - aa, i], send.at[i], recv.at[i], dev_x
+        )
+
+    def wide(ref, i):
+        return jnp.concatenate([ref[0, i], ref[1, i]], axis=1).astype(F32)
+
+    def put(ref, i, rows):
+        rows = rows.astype(BF16)
+        ref[0, i] = rows[:, :half]
+        ref[1, i] = rows[:, half:]
 
     cols = 2 * piece
     parts = w1_own.shape[1] // cols
@@ -218,7 +222,6 @@
     w2_copy.start()
     y2b[...] = jnp.zeros(y2b.shape, BF16)
     gb[...] = jnp.zeros(gb.shape, BF16)
-    rs[0] = jnp.zeros(rs.shape[1:], BF16)
     vacc[...] = jnp.zeros(vacc.shape, F32)
     small[...] = jnp.zeros(small.shape, F32)
     t1v[...] = column(tb1[...], t1v.shape[0])
@@ -257,7 +260,12 @@
         def _():
             give(cot, cb, snd_c, rcv_c, i + LOOK - imgs).start()
 
-        x = xb[i].astype(F32)
+        @pl.when(i == imgs - 1)
+        def _():
+            for n in range(LOOK, imgs):
+                give(cot, cb, snd_c, rcv_c, n).start()
+
+        x = wide(xb, i)
         mean = jnp.mean(x, -1, keepdims=True)
         xc = x - mean
         rstd = lax.rsqrt(jnp.mean(xc * xc, -1, keepdims=True) + EPS)
@@ -323,43 +331,34 @@
             return carry
 
         lax.fori_loop(0, RING // 2, two, 0)
-
-        def three(k, carry):
-            i = chunk * each + k
-            rows = pl.ds(pl.multiple_of(i * pad, 16), patches)
-            ob[i] = (weight(i) * (res[i] + acc[rows, :] + vec(4))).astype(BF16)
-            return carry
-
-        lax.fori_loop(0, each, three, 0)
         return carry
 
     lax.fori_loop(0, chunks, forward_chunk, 0)
-    for i in range(LOOK, imgs):
-        give(cot, cb, snd_c, rcv_c, i).start()
+    def out_local(i):
+        return pltpu.make_async_copy(cb.at[aa, i], out_o.at[aa * imgs + i], loc_o.at[i])
+
+    def out_remote(i, sender):
+        return remote(
+            cb.at[1 - aa, i], out_o.at[sender * imgs + i], snd_o.at[i], rcv_o.at[i], dev_x
+        )
 
     def mask_cot(i, carry):
         local_in(cot, cb, loc_c, i).wait()
         take(cot, cb, snd_c, rcv_c, i).wait()
         rows = pl.ds(pl.multiple_of(i * pad, 16), patches)
-        gb[rows, :] = (cb[i].astype(F32) * weight(i)).astype(BF16)
+        scale = weight(i)
+        gb[rows, :] = (wide(cb, i) * scale).astype(BF16)
+        put(cb, i, scale * (res[i] + acc[rows, :] + vec(4)))
         return carry
 
     lax.fori_loop(0, imgs, mask_cot, 0)
 
-    def out_local(i):
-        return pltpu.make_async_copy(ob.at[i, :, mine], out_o.at[aa * imgs + i], loc_o.at[i])
-
-    def out_remote(i, sender):
-        return remote(
-            ob.at[i, :, other], out_o.at[sender * imgs + i], snd_o.at[i], rcv_o.at[i], dev_x
-        )
-
     def grad_local(i):
-        return pltpu.make_async_copy(xb.at[i, :, mine], gim_o.at[aa * imgs + i], loc_i.at[i])
+        return pltpu.make_async_copy(xb.at[aa, i], gim_o.at[aa * imgs + i], loc_i.at[i])
 
     def grad_remote(i, sender):
         return remote(
-            xb.at[i, :, other], gim_o.at[sender * imgs + i], snd_i.at[i], rcv_i.at[i], dev_x
+            xb.at[1 - aa, i], gim_o.at[sender * imgs + i], snd_i.at[i], rcv_i.at[i], dev_x
         )
 
     ones = jnp.ones((8, chans), BF16)
@@ -379,7 +378,7 @@
         grad_res = grad_out + rstd * (q - mean - normed * proj)
         grad_tok = grad_res.astype(BF16)
         rstd = stat[i, :, 1 : 2]
-        normed = (xb[i].astype(F32) - stat[i, :, 0 : 1]) * rstd
+        normed = (wide(xb, i) - stat[i, :, 0 : 1]) * rstd
         y1 = (normed * vec(0) + vec(1)).astype(BF16)
         val, der = gelu_both(dot(tw1[...], y1, 0, 0) + t1v[...])
         small[200 : 200 + patches, :] += dot(grad_tok, val.astype(BF16), 1, 1)
@@ -393,21 +392,20 @@
         q = up * vec(0)
         mean = jnp.mean(q, -1, keepdims=True)
         proj = jnp.mean(q * normed, -1, keepdims=True)
-        xb[i] = (grad_res + rstd * (q - mean - normed * proj)).astype(BF16)
+        put(xb, i, grad_res + rstd * (q - mean - normed * proj))
         grad_local(i).start()
         grad_remote(i, aa).start()
 
     bars = bar.shape[0]
     solo_mine = pl.ds(pl.multiple_of(aa * SOLO, 16), SOLO)
     solo_other = pl.ds(pl.multiple_of((1 - aa) * SOLO, 16), SOLO)
-    shared = pl.ds(2 * SOLO, both)
 
     def own_rows(place, size):
         return pl.ds(pl.multiple_of(ba * piece + place, 16), size)
 
-    def to_core(s, a):
+    def to_core(s, par, a):
         return remote(
-            pb.at[lax.rem(s, 2), a, rows_other, :],
+            pb.at[par, a, rows_other, :],
             bar.at[lax.rem(s, bars), a],
             snd_b.at[lax.rem(s, bars), a],
             rcv_b.at[lax.rem(s, bars), a],
@@ -415,15 +413,20 @@
         )
 
     def to_x(s, a):
+        slot = lax.rem(s, bars)
         return remote(
-            bar.at[lax.rem(s, bars), a, solo_other, :],
-            xr.at[lax.rem(s, 2), a],
-            snd_h.at[lax.rem(s, 2), a],
-            rcv_h.at[lax.rem(s, 2), a],
+            bar.at[slot, a, solo_other, :],
+            xr.at[slot, a],
+            snd_h.at[slot, a],
+            rcv_h.at[slot, a],
             dev_x,
         )
 
-    ring_rows = (pl.ds(0, SOLO), pl.ds(SOLO, both))
+    part = both // 2
+    ring_rows = (pl.ds(0, SOLO), pl.ds(SOLO, part), pl.ds(SOLO + part, part))
+    own_at = (aa * SOLO, 2 * SOLO, 2 * SOLO + part)
+    order = (1, 2, 0)
+    last = RING - 1
 
     def to_ring(s, a, c):
         return remote(
@@ -434,92 +437,139 @@
             dev_ring[a],
         )
 
-    def first_sum(s, a):
-        to_core(s, a).wait_recv()
+    def swap(a, c):
+        src = rs.at[last, a, ring_rows[c], :]
+        dst = fs.at[a, solo_mine, :] if c == 0 else xs.at[a, pl.ds((c - 1) * part, part), :]
+        return remote(src, dst, snd_e.at[0, a, c], rcv_e.at[0, a, c], dev_x)
+
+    def first_sum(s, par, wait=True):
         slot = lax.rem(s, bars)
-        own = own_rows((1 - aa) * SOLO, SOLO)
-        total = pb[lax.rem(s, 2), a, own, :].astype(F32) + bar[slot, a, solo_other, :].astype(F32)
-        bar[slot, a, solo_other, :] = total.astype(BF16)
-        to_x(s, a).start()
-
-    def second_sum(s, a):
-        par = lax.rem(s, 2)
+        for a in range(2):
+            if wait:
+                to_core(s, par, a).wait_recv()
+            own = own_rows((1 - aa) * SOLO, SOLO)
+            total = pb[par, a, own, :].astype(F32) + bar[slot, a, solo_other, :].astype(F32)
+            bar[slot, a, solo_other, :] = total.astype(BF16)
+            to_x(s, a).start()
+            own = own_rows(aa * SOLO, SOLO)
+            held[par, a] = pb[par, a, own, :].astype(F32) + bar[slot, a, solo_mine, :].astype(F32)
+
+    def pass_sum(s, a, c, total, first, final):
+        if not first:
+            to_ring(s - 1, a, c).wait_recv()
+            total = total + rs[s, a, ring_rows[c], :].astype(F32)
+        total = total.astype(BF16)
+        rs[s, a, ring_rows[c], :] = total
+        if not final:
+            to_ring(s, a, c).start()
+        else:
+            if c == 0:
+                fs[a, solo_mine, :] = total
+            swap(a, c).start()
+
+    def shared_sum(s, par, a, first=False, final=False):
         slot = lax.rem(s, bars)
-        for c in (1, 0):
-            if c == 0:
-                to_x(s, a).wait()
-
-            @pl.when(s > 0)
-            def _():
-                to_ring(s - 1, a, c).wait_recv()
-
-            if c == 0:
-                more = (
-                    pb[par, a, own_rows(aa * SOLO, SOLO), :].astype(F32)
-                    + bar[slot, a, solo_mine, :].astype(F32)
-                    + xr[par, a].astype(F32)
-                )
-            else:
-                more = pb[par, a, own_rows(2 * SOLO, both), :].astype(F32) + bar[
-                    slot, a, shared, :
-                ].astype(F32)
-            rs[s, a, ring_rows[c], :] = (rs[s, a, ring_rows[c], :].astype(F32) + more).astype(BF16)
-
-            @pl.when(s < RING - 1)
-            def _():
-                to_ring(s, a, c).start()
-
-    def chan_backward(j, carry):
-        @pl.when(j < RING)
-        def _():
-            par = lax.rem(j, 2)
-
-            @pl.when(j >= 2)
-            def _():
-                for a in range(2):
-                    to_core(j - 2, a).wait_send()
-
-            pb[par, 0] = dot(act[mod(pos - 1 - j)], gb[...], 0, 0).astype(BF16)
-            to_core(j, 0).start()
-
-        @pl.when(j > 0)
-        def _():
-            for a in range(2):
-                first_sum(j - 1, a)
-
-        @pl.when(j < RING)
-        def _():
-            left = mod(pos + 1 + j)
-            grad = (dot(gb[...], w2b[left], 1, 1) * dg[left].astype(F32)).astype(BF16)
-            small[pl.ds(416 + left, 1), :] = jnp.sum(grad.astype(F32), 0, keepdims=True)
-            pb[lax.rem(j, 2), 1] = dot(grad, y2b[...], 0, 0).astype(BF16)
-            to_core(j, 1).start()
-            acc[...] = jnp.where(j == 0, 0.0, acc[...]) + dot(grad, w1b[left], 1, 0)
-
-        @pl.when(j == RING)
-        def _():
-            token_backward(0)
-
-        @pl.when(j > 0)
-        def _():
-            for a in range(2):
-                second_sum(j - 1, a)
-
-        @pl.when(j < imgs)
-        def _():
-            out_local(j).start()
-            out_remote(j, aa).start()
-
+        for c in (1, 2):
+            total = pb[par, a, own_rows(own_at[c], part), :].astype(F32)
+            total = total + bar[slot, a, pl.ds(own_at[c], part), :].astype(F32)
+            pass_sum(s, a, c, total, first, final)
+
+    def solo_sum(s, par, first=False, final=False):
+        for a in range(2):
+            to_x(s, a).wait()
+            total = held[par, a] + xr[lax.rem(s, bars), a].astype(F32)
+            pass_sum(s, a, 0, total, first, final)
+
+    def lefts(k):
+        return mod(pos + 1 + 2 * k), mod(pos + 2 + 2 * k)
+
+    def grad_hidden(k):
+        pair = lefts(k)
+        rows = jnp.concatenate([w2b[n] for n in pair], axis=0)
+        slope = jnp.concatenate([dg[n] for n in pair], axis=1).astype(F32)
+        grad = (dot(gb[...], rows, 1, 1) * slope).astype(BF16)
+        total = jnp.sum(grad.astype(F32), 0, keepdims=True)
+        for n, left in enumerate(pair):
+            dg[left] = grad[:, n * cols : (n + 1) * cols]
+            small[pl.ds(416 + left, 1), :] = total[:, n * cols : (n + 1) * cols]
+
+    def grad_rows(k, first=False):
+        pair = lefts(k)
+        grad = jnp.concatenate([dg[n] for n in pair], axis=1)
+        new = dot(grad, jnp.concatenate([w1b[n] for n in pair], axis=0), 1, 0)
+        acc[...] = new if first else acc[...] + new
+
+    def weight_out(j, par):
+        pb[par, 0] = dot(act[mod(pos - 1 - j)], gb[...], 0, 0).astype(BF16)
+        to_core(j, par, 0).start()
+
+    def weight_in(j, par):
+        pb[par, 1] = dot(dg[mod(pos + 1 + j)], y2b[...], 0, 0).astype(BF16)
+        to_core(j, par, 1).start()
+
+    def sent_to_core(j, par):
+        for a in range(2):
+            to_core(j, par, a).wait_send()
+
+    def send_out(i):
+        out_local(i).start()
+        out_remote(i, aa).start()
+
+    weight_out(0, 0)
+    grad_hidden(0)
+    weight_in(0, 0)
+    to_core(0, 0, 0).wait_recv()
+    shared_sum(0, 0, 0, first=True)
+    weight_out(1, 1)
+    to_core(0, 0, 1).wait_recv()
+    shared_sum(0, 0, 1, first=True)
+    first_sum(0, 0, wait=False)
+    weight_in(1, 1)
+    grad_hidden(1)
+    first_sum(1, 1)
+
+    def chan_backward(k, carry):
+        sent_to_core(2 * k - 2, 0)
+        weight_out(2 * k, 0)
+        weight_in(2 * k, 0)
+        shared_sum(2 * k - 1, 1, 0)
+        shared_sum(2 * k - 1, 1, 1)
+
+        @pl.when(k == 1)
+        def _():
+            solo_sum(0, 0, first=True)
+            grad_rows(0, first=True)
+
+        @pl.when(k > 1)
+        def _():
+            solo_sum(2 * k - 2, 0)
+            grad_rows(k - 1)
+
+        send_out(2 * k - 2)
+        first_sum(2 * k, 0)
+        sent_to_core(2 * k - 1, 1)
+        weight_out(2 * k + 1, 1)
+        weight_in(2 * k + 1, 1)
+        shared_sum(2 * k, 0, 0)
+        shared_sum(2 * k, 0, 1)
+        solo_sum(2 * k - 1, 1)
+        send_out(2 * k - 1)
+
+        @pl.when(k + 1 < RING // 2)
+        def _():
+            grad_hidden(k + 1)
+
+        @pl.when(k + 1 == RING // 2)
+        def _():
+            grad_rows(k)
+
+        first_sum(2 * k + 1, 1)
         return carry
 
-    lax.fori_loop(0, RING + 1, chan_backward, 0)
-    for s in (RING - 2, RING - 1):
-        for a in range(2):
-            to_core(s, a).wait_send()
-
-    last = RING - 1
+    lax.fori_loop(1, RING // 2, chan_backward, 0)
+
     results = (d2_o, d1_o)
-    gather_rows = (solo_mine, shared)
+    gather_rows = (pl.ds(0, 2 * SOLO), pl.ds(2 * SOLO, part), pl.ds(2 * SOLO + part, part))
 
     def gather(t, a, c, src):
         q = mod(pos - t) if a == 0 else mod(pos + t)
@@ -533,80 +583,76 @@
         dst = results[a].at[q, gather_rows[c], :]
         return remote(dst, dst, snd_g.at[t, a, c], rcv_g.at[t, a, c], dev_ring[a])
 
-    def across(t, a, src):
-        q = mod(pos - t) if a == 0 else mod(pos + t)
-        dst = results[a].at[q, solo_mine, :]
-        return remote(dst if src is None else src, dst, snd_f.at[t, a], rcv_f.at[t, a], dev_x)
-
-    def across_arrival(t, a):
-        q = mod(pos - t) if a == 0 else mod(pos + t)
-        dst = results[a].at[q, solo_other, :]
-        return remote(dst, dst, snd_f.at[t, a], rcv_f.at[t, a], dev_x)
-
-    def add_hi(c):
-        for k, dev in enumerate(dev_hi):
-            for a in range(2):
-                src = rs.at[last, a, ring_rows[c], :]
-                landed = xh.at[k, a, ring_rows[c], :]
-                near = pb.at[0, 0, ring_rows[c], :]
+    def keep(a, c):
+        return pltpu.make_async_copy(
+            fs.at[a, gather_rows[c], :], results[a].at[pos, gather_rows[c], :], loc_g.at[a, c]
+        )
+
+    def start_gather(c):
+        for a in range(2):
+            rows = gather_rows[c]
+            swap(a, c).wait_send()
+            if c == 0:
+                remote(
+                    fs.at[a, solo_mine, :],
+                    fs.at[a, solo_other, :],
+                    snd_e.at[0, a, c],
+                    rcv_e.at[0, a, c],
+                    dev_x,
+                ).wait_recv()
+            else:
+                swap(a, c).wait_recv()
+                fs[a, rows, :] = (
+                    rs[last, a, ring_rows[c], :].astype(F32)
+                    + xs[a, (c - 1) * part : c * part, :].astype(F32)
+                ).astype(BF16)
+            for k, dev in enumerate(dev_hi):
+                src = fs.at[a, rows, :]
+                landed = xh.at[k, a, rows, :]
+                near = pb.at[0, 0, rows, :]
                 copy = remote(src, landed, snd_e.at[1 + k, a, c], rcv_e.at[1 + k, a, c], dev)
                 copy.start()
                 copy.wait()
                 back = pltpu.make_async_copy(landed, near, loc_g.at[a, c])
                 back.start()
                 back.wait()
-                rs[last, a, ring_rows[c], :] = (
-                    rs[last, a, ring_rows[c], :].astype(F32) + pb[0, 0, ring_rows[c], :].astype(F32)
+                fs[a, rows, :] = (
+                    fs[a, rows, :].astype(F32) + pb[0, 0, rows, :].astype(F32)
                 ).astype(BF16)
-
-    keep = []
-
-    def start_gather(c):
-        add_hi(c)
-        for a in range(2):
-            src = rs.at[last, a, ring_rows[c], :]
-            gather(0, a, c, src).start()
-            if c == 0:
-                across(0, a, src).start()
-            keep.append(
-                pltpu.make_async_copy(
-                    src, results[a].at[pos, gather_rows[c], :], loc_g.at[a, c]
-                )
-            )
-            keep[-1].start()
-
-    swaps = [
-        remote(rs.at[last, a, ring_rows[1], :], xs.at[a], snd_e.at[0, a, 1], rcv_e.at[0, a, 1], dev_x)
-        for a in range(2)
-    ]
-    for copy in swaps:
-        copy.start()
-    start_gather(0)
-    token_backward(1)
-    for a, copy in enumerate(swaps):
-        copy.wait()
-        total = rs[last, a, ring_rows[1], :].astype(F32) + xs[a].astype(F32)
-        rs[last, a, ring_rows[1], :] = total.astype(BF16)
-    start_gather(1)
+            gather(0, a, c, fs.at[a, rows, :]).start()
+            keep(a, c).start()
 
     def pass_on(t):
-        for c in range(2):
+        for c in order:
             for a in range(2):
                 gather_arrival(t, a, c).wait_recv()
-
-                @pl.when(t + 1 < RING - 1)
-                def _():
+                if t + 1 < RING - 1:
                     gather(t + 1, a, c, None).start()
 
-                if c == 0:
-                    across(t + 1, a, None).start()
-
-    def token_and_gather(t, carry):
-        token_backward(t + 2)
-        pass_on(t)
+    def token_and_gather(i, carry):
+        token_backward(i)
+
+        @pl.when(i == 0)
+        def _():
+            sent_to_core(RING - 2, 0)
+            sent_to_core(last, 1)
+            for a in range(2):
+                shared_sum(last, 1, a, final=True)
+            solo_sum(RING - 2, 0)
+            solo_sum(last, 1, final=True)
+
+        @pl.when(i == 1)
+        def _():
+            start_gather(1)
+
+        @pl.when(i == 3)
+        def _():
+            start_gather(2)
+            start_gather(0)
+
         return carry
 
-    lax.fori_loop(0, imgs - 2, token_and_gather, 0)
+    lax.fori_loop(0, imgs, token_and_gather, 0)
     small[424:432, :] = vacc[:, :half]
     small[432:440, :] = vacc[:, half:]
 
@@ -656,20 +702,19 @@
             remote(region, region, snd_s.at[n], rcv_s.at[n], dev_x).wait_recv()
 
     small_start(0)
-    done = 0
-    for t in range(imgs - 2, RING - 1):
+    for t in range(RING - 1):
         pass_on(t)
-        small_finish(done)
-        done += 1
-        small_start(done)
-    while done < len(small_steps):
-        small_finish(done)
-        done += 1
-        if done < len(small_steps):
-            small_start(done)
-
-    for copy in keep:
-        copy.wait()
+        small_finish(t)
+        if t + 1 < len(small_steps):
+            small_start(t + 1)
+    for n in range(RING - 1, len(small_steps)):
+        small_finish(n)
+        if n + 1 < len(small_steps):
+            small_start(n + 1)
+
+    for a in range(2):
+        for c in range(3):
+            keep(a, c).wait()
 
     def drain_images(i, carry):
         out_local(i).wait()
@@ -682,17 +727,12 @@
 
     def drain_ring(t, carry):
         for a in range(2):
-            across_arrival(t, a).wait()
-
-            @pl.when(t < RING - 1)
-            def _():
-                for c in range(2):
-                    to_ring(t, a, c).wait_send()
-                    gather_arrival(t, a, c).wait_send()
-
+            for c in range(3):
+                to_ring(t, a, c).wait_send()
+                gather_arrival(t, a, c).wait_send()
         return carry
 
-    lax.fori_loop(0, RING, drain_ring, 0)
+    lax.fori_loop(0, RING - 1, drain_ring, 0)
 
 
 def finish_kernel(gim, d2, d1, small, gim_o, w2_o, w1_o, tw1_o, tw2_o, tb1_o, tb2_o, b1_o, *vec_o):
@@ -746,7 +786,7 @@
             jax.ShapeDtypeStruct((RING, piece, chans), BF16),
             jax.ShapeDtypeStruct((RING, piece, chans), BF16),
             jax.ShapeDtypeStruct((total, hid_tok), BF16),
-            jax.ShapeDtypeStruct((his, 2, keep_rows if groups > 1 else 16, chans), BF16),
+            jax.ShapeDtypeStruct((his, 2, piece if groups > 1 else 16, chans), BF16),
         ],
         in_specs=[pl.BlockSpec(memory_space=pltpu.SMEM), hbm, hbm]
         + [vmem] * 9
@@ -754,9 +794,8 @@
         + [vmem],
         out_specs=[hbm] * 4 + [vmem, hbm],
         scratch_shapes=[
-            pltpu.VMEM((imgs, patches, chans), BF16),
-            pltpu.VMEM((imgs, patches, chans), BF16),
-            pltpu.VMEM((imgs, patches, chans), BF16),
+            pltpu.VMEM((2, imgs, patches, half), BF16),
+            pltpu.VMEM((2, imgs, patches, half), BF16),
             pltpu.VMEM((imgs * pad, chans), BF16),
             pltpu.VMEM((imgs * pad, chans), BF16),
             pltpu.VMEM((imgs, patches, chans), F32),
@@ -768,9 +807,11 @@
             pltpu.VMEM((imgs, patches, 4), F32),
             pltpu.VMEM((2, 2, 2 * piece, chans), BF16),
             pltpu.VMEM((4, 2, piece, chans), BF16),
-            pltpu.VMEM((2, 2, SOLO, chans), BF16),
+            pltpu.VMEM((4, 2, SOLO, chans), BF16),
+            pltpu.VMEM((2, 2, SOLO, chans), F32),
             pltpu.VMEM((RING, 2, keep_rows, chans), BF16),
             pltpu.VMEM((2, both, chans), BF16),
+            pltpu.VMEM((2, piece, chans), BF16),
             pltpu.VMEM((2, 8, half), F32),
             pltpu.VMEM((2, 1, hidden), F32),
             pltpu.VMEM((RING, 2 * piece), F32),
@@ -789,17 +830,15 @@
             dma((4,)),
             dma((4, 2)),
             dma((4, 2)),
-            dma((2, 2)),
-            dma((2, 2)),
-            dma((RING, 2, 2)),
-            dma((RING, 2, 2)),
-            dma((1 + his, 2, 2)),
-            dma((1 + his, 2, 2)),
-            dma((RING, 2, 2)),
-            dma((RING, 2, 2)),
-            dma((RING, 2)),
-            dma((RING, 2)),
-            dma((2, 2)),
+            dma((4, 2)),
+            dma((4, 2)),
+            dma((RING, 2, 3)),
+            dma((RING, 2, 3)),
+            dma((1 + his, 2, 3)),
+            dma((1 + his, 2, 3)),
+            dma((RING, 2, 3)),
+            dma((RING, 2, 3)),
+            dma((2, 3)),
             *per_image,
             *per_image,
             dma((4 + flies,)),

time: 199 us -> 181 us (0.910)
  Pallas kernels: 196 us -> 178 us
    pallas_call x1, Pallas kernels: 187 us -> 169 us  [local(): pl.pallas_call(functools.partial(layer_kernel, groups), out_shape=[jax.Sh...]
where the time goes in v3:
time: 181 us
  Pallas kernels  178 us (98%)
    pallas_call x1, Pallas kernels, local(): pl.pallas_call(functools.partial(layer_kernel, groups), out_shape=[jax.Sh...  169 us
    pallas_call x1, Pallas kernels, local(): pl.pallas_call(finish_kernel, grid=(steps,), out_shape=[jax.ShapeDtypeStr...  8.8 us

profile of v3, /device:TPU:0, one launch (start us, length us, event | category | flops | bytes accessed | tf_op | source)
XLA Modules:
  0.0 180.7 jit_solution(14079267271680427617)
XLA Ops:
  1.3 169.3 %shard_map.254 = (bf16[12,196,384]{2,1,0:T(8,128)(2,1)}, bf16[12,196,384]{2,1,0:T(8,128)(2,1)}, bf16[8,192,768]{2,1,0:T(8,128)(2,1)}, bf16[8,192,768]{2,1,0:T(8,...) custom-call(s32[1]{0:T(128)S(6)} %copy.30.counts, bf16[12,196,384]{2,1,0:T(8,128)(2,1)} %images.1, ...), custom_call_target="tpu_custom_call" | custom-call | tf_op jit(solution)/shard_map/pallas_call | solution.py:781
  170.6 0.0 copy-start
  170.6 8.8 %shard_map.255 = (f32[12,196,384]{2,1,0:T(8,128)}, f32[1536,768]{1,0:T(8,128)}, f32[768,1536]{1,0:T(8,128)}, f32[196,384]{1,0:T(8,128)}, f32[196,384]{1,0:T(8,12...) custom-call(bf16[12,196,384]{2,1,0:T(8,128)(2,1)} %get-tuple-element, ...), custom_call_target="tpu_custom_call" | custom-call | tf_op jit(solution)/shard_map/pallas_call | solution.py:875
  179.4 0.0 copy-done
  179.4 1.2 copy.31
Async XLA Ops:
  170.6 8.8 %copy-start = (bf16[12,196,384]{2,1,0:T(8,128)(2,1)S(1)}, bf16[12,196,384]{2,1,0:T(8,128)(2,1)}, u32[]{:S(2)}) copy-start(bf16[12,196,384]{2,1,0:T(8,128)(2,1)} %get-tuple-element.64) | copy-start | bytes 5419012
